TPU v7x, 32 devices: a whole 2x2x4 slice. The times are simulated.
32 devices in a mesh: img: 8 (over z, core), txt: 4 (over y, x).
Axes of the slice: x: 2, y: 2, z: 4, core: 2. Of those that a mesh axis runs over, the one named last changes fastest.
Arguments:
- image_feats: bfloat16 [512, 768], P(('img', 'txt')), may hold values from -6 to 6
- text_feats: bfloat16 [512, 512], P(('txt', 'img')), may hold values from -6 to 6
- teacher_img: bfloat16 [512, 1024], P(('img', 'txt')), may hold values from -60 to 60, as said below
- teacher_txt: bfloat16 [512, 1024], P(('txt', 'img')), may hold values from -60 to 60, as said below
- proj_img: bfloat16 [768, 512], replicated, may hold values from -0.21875 to 0.21875
- proj_txt: bfloat16 [512, 512], replicated, may hold values from -0.25 to 0.25
Outputs:
- loss: float32 [], replicated
- grad_img: float32 [768, 512], replicated
- grad_txt: float32 [512, 512], replicated
Inputs may be any that keep to these rules, and one draw needn't show every extreme that they name: `teacher_img`: raw teacher embeddings, rows of various scales. `teacher_txt`: raw teacher embeddings, rows of various scales.
All inputs are finite; a program needn't handle non-finite values.
Results may differ from a plain program's by a relative error of at most 0.0077.
Values may be sent and summed in bfloat16 or wider, within the bound.
A program may use at most 64 MiB of HBM per device.

v0:
```python
import jax
import jax.numpy as jnp
from jax import lax
from jax.sharding import PartitionSpec as P

EPS = 1e-06
TEACHER_SCALE = 100.0
STUDENT_SCALE = 50.0


def project(feats, weight):
    u = jnp.dot(feats, weight, preferred_element_type=jnp.float32)
    inv = lax.rsqrt(jnp.sum(u * u, axis=1, keepdims=True) + EPS)
    return (u * inv, inv)


def normed(raw):
    x = raw.astype(jnp.float32)
    return (x * lax.rsqrt(jnp.sum(x * x, axis=1, keepdims=True) + EPS)).astype(jnp.bfloat16)


def tangent(grad_rows, embeds, inverse):
    return (grad_rows - embeds * jnp.sum(embeds * grad_rows, 1, keepdims=True)) * inverse


def weight_grad(feats, du_rows):
    return lax.dot_general(
        feats.astype(jnp.float32),
        du_rows,
        (((0,), (0,)), ((), ())),
        precision=lax.Precision.HIGHEST,
    )


def tile_terms(block_q_img, block_q_txt, block_s_img, block_s_txt):
    tl = TEACHER_SCALE * jnp.dot(block_q_img, block_q_txt.T, preferred_element_type=jnp.float32)
    sl = STUDENT_SCALE * jnp.dot(block_s_img, block_s_txt.T, preferred_element_type=jnp.float32)
    rtm, rsm = lax.pmax((tl.max(1), sl.max(1)), "txt")
    rts, rss = lax.psum(
        (jnp.sum(jnp.exp(tl - rtm[:, None]), 1), jnp.sum(jnp.exp(sl - rsm[:, None]), 1)), "txt"
    )
    ctm, csm = lax.pmax((tl.max(0), sl.max(0)), "img")
    cts, css = lax.psum(
        (jnp.sum(jnp.exp(tl - ctm[None, :]), 0), jnp.sum(jnp.exp(sl - csm[None, :]), 0)), "img"
    )
    pt_row = jnp.exp(tl - rtm[:, None]) / rts[:, None]
    ps_row = jnp.exp(sl - rsm[:, None]) / rss[:, None]
    pt_col = jnp.exp(tl - ctm[None, :]) / cts[None, :]
    ps_col = jnp.exp(sl - csm[None, :]) / css[None, :]
    diff = tl - sl
    n_img = lax.axis_size("img")
    n_txt = lax.axis_size("txt")
    local_term = jnp.sum(pt_row * diff) + jnp.sum(pt_col * diff)
    local_term = local_term + jnp.sum(rsm + jnp.log(rss) - rtm - jnp.log(rts)) / n_txt
    local_term = local_term + jnp.sum(csm + jnp.log(css) - ctm - jnp.log(cts)) / n_img
    grad_tile = (0.5 * STUDENT_SCALE * (ps_row - pt_row + (ps_col - pt_col))).astype(jnp.bfloat16)
    part_img = jnp.dot(grad_tile, block_s_txt, preferred_element_type=jnp.float32)
    part_txt = lax.dot_general(
        grad_tile, block_s_img, (((0,), (0,)), ((), ())), preferred_element_type=jnp.float32
    )
    return (part_img, part_txt, local_term)


def shards(image_feats, text_feats, teacher_img, teacher_txt, proj_img, proj_txt):
    e_img, inv_img = project(image_feats, proj_img)
    e_txt, inv_txt = project(text_feats, proj_txt)
    q_img = normed(teacher_img)
    q_txt = normed(teacher_txt)
    feats_img, block_q_img = (
        lax.all_gather(image_feats, "txt", axis=0, tiled=True),
        lax.all_gather(q_img, "txt", axis=0, tiled=True),
    )
    feats_txt, block_q_txt = (
        lax.all_gather(text_feats, "img", axis=0, tiled=True),
        lax.all_gather(q_txt, "img", axis=0, tiled=True),
    )
    block_s_img = project(feats_img, proj_img)[0].astype(jnp.bfloat16)
    block_s_txt = project(feats_txt, proj_txt)[0].astype(jnp.bfloat16)
    part_img, part_txt, local_term = tile_terms(block_q_img, block_q_txt, block_s_img, block_s_txt)
    d_img = lax.psum_scatter(part_img, "txt", scatter_dimension=0, tiled=True)
    d_txt = lax.psum_scatter(part_txt, "img", scatter_dimension=0, tiled=True)
    local_img = weight_grad(image_feats, tangent(d_img, e_img, inv_img))
    local_txt = weight_grad(text_feats, tangent(d_txt, e_txt, inv_txt))
    grad_img, grad_txt, total = lax.psum((local_img, local_txt, local_term), ("img", "txt"))
    batch_total = image_feats.shape[0] * lax.axis_size("img") * lax.axis_size("txt")
    loss = total / (2.0 * batch_total)
    return (loss, grad_img, grad_txt)


def solution(mesh):
    return jax.shard_map(
        shards,
        mesh=mesh,
        in_specs=(
            P(("img", "txt"), None),
            P(("txt", "img"), None),
            P(("img", "txt"), None),
            P(("txt", "img"), None),
            P(),
            P(),
        ),
        out_specs=(P(), P(), P()),
        check_vma=False,
    )
```

profile of v0, /device:TPU:0, one launch (start us, length us, event | category | flops | bytes accessed | tf_op | source)
XLA Modules:
  0.0 327.6 jit_solution(12125367819099392428)
XLA Ops:
  7.2 0.0 copy-start
  7.2 0.0 copy-start.1
  7.2 0.0 reduce-scatter.3.cloned.1.call-start
  7.2 1.0 fusion
  8.2 0.9 fusion.2
  9.1 0.8 fusion.3
  9.9 0.8 fusion.1
  10.8 9.9 %all_gather.12 = bf16[64,1024]{1,0:T(8,128)(2,1)S(1)} all-gather(bf16[16,1024]{1,0:T(8,128)(2,1)S(1)} %fusion.1), channel_id=1, replica_groups=mesh['img'=8,'txt'=4] {'txt'}, dimensions={0}, use_global_device_ids=true | all-gather | bytes 163840 | tf_op jit(solution)/shard_map/all_gather | solution.py:71
  20.7 8.3 %all_gather.14 = bf16[64,768]{1,0:T(8,128)(2,1)S(1)} all-gather(bf16[16,768]{1,0:T(8,128)(2,1)} %param.6), channel_id=1, replica_groups=mesh['img'=8,'txt'=4] {'txt'}, dimensions={0}, use_global_device_ids=true | all-gather | bytes 122880 | tf_op jit(solution)/shard_map/all_gather | solution.py:70
  29.0 0.0 copy-done
  29.0 0.3 multiply_reduce_fusion.1
  29.4 14.5 %all_gather.15 = bf16[128,512]{1,0:T(8,128)(2,1)S(1)} all-gather(bf16[16,512]{1,0:T(8,128)(2,1)} %param.7), channel_id=1, replica_groups=mesh['img'=8,'txt'=4] {'img'}, dimensions={0}, use_global_device_ids=true | all-gather | bytes 147456 | tf_op jit(solution)/shard_map/all_gather | solution.py:74
  43.9 0.3 multiply_reduce_fusion
  44.2 0.0 copy-start.3
  44.2 14.2 %all_gather.13 = bf16[128,1024]{1,0:T(8,128)(2,1)S(1)} all-gather(bf16[16,1024]{1,0:T(8,128)(2,1)S(1)} %fusion.3), channel_id=1, replica_groups=mesh['img'=8,'txt'=4] {'img'}, dimensions={0}, use_global_device_ids=true | all-gather | bytes 294912 | tf_op jit(solution)/shard_map/all_gather | solution.py:75
  58.4 0.3 fusion.25
  58.7 0.0 copy-start.4
  58.7 0.3 fusion.26
  59.0 8.9 %all-reduce.3 = (f32[64]{0:T(128)S(1)}, f32[64]{0:T(128)S(1)}) all-reduce(f32[64]{0:T(128)S(1)} %get-tuple-element.28, f32[64]{0:T(128)S(1)} %get-tuple-element.14), channel_id=1, replica_groups=mesh['img'=8,'txt'=4] {'txt'}, use_global_device_ids=true, to_apply=%region_15.0 | all-reduce | flops 128 | bytes 1024 | tf_op jit(solution)/shard_map/pmax | solution.py:38
  68.0 0.2 fusion.24
  68.1 14.9 %all-reduce.1 = (f32[128]{0:T(128)S(1)}, f32[128]{0:T(128)S(1)}) all-reduce(f32[128]{0:T(128)S(1)} %get-tuple-element.13, f32[128]{0:T(128)S(1)} %get-tuple-element.9), channel_id=1, replica_groups=mesh['img'=8,'txt'=4] {'img'}, use_global_device_ids=true, to_apply=%region_10.0 | all-reduce | flops 256 | bytes 2048 | tf_op jit(solution)/shard_map/pmax | solution.py:42
  83.1 0.2 fusion.15
  83.3 13.6 %psum.50 = f32[128]{0:T(128)S(1)} all-reduce(f32[128]{0:T(128)S(1)} %get-tuple-element.11), channel_id=1, replica_groups=mesh['img'=8,'txt'=4] {'img'}, use_global_device_ids=true, to_apply=%region_12.0 | all-reduce | flops 128 | bytes 1024 | tf_op jit(solution)/shard_map/psum | solution.py:43
  96.8 8.1 %all-reduce.2 = (f32[64]{0:T(128)S(1)}, f32[64]{0:T(128)S(1)}) all-reduce(f32[64]{0:T(128)S(1)} %get-tuple-element.12, f32[64]{0:T(128)S(1)} %get-tuple-element.10), channel_id=1, replica_groups=mesh['img'=8,'txt'=4] {'txt'}, use_global_device_ids=true, to_apply=%region_5.0 | all-reduce | flops 128 | bytes 1024 | tf_op jit(solution)/shard_map/psum | solution.py:39
  105.0 0.7 multiply_reduce_fusion.6
  105.7 13.6 %psum.52 = f32[128]{0:T(128)S(1)} all-reduce(f32[128]{0:T(128)S(1)} %get-tuple-element.8), channel_id=1, replica_groups=mesh['img'=8,'txt'=4] {'img'}, use_global_device_ids=true, to_apply=%region_22.0 | all-reduce | flops 128 | bytes 1024 | tf_op jit(solution)/shard_map/psum | solution.py:43
  119.2 0.9 fusion.23
  120.2 0.0 reduce-scatter.3.cloned.1.call-update
  120.2 0.0 reduce-scatter.5.cloned.1.call-start
  120.2 1.0 fusion.22
  121.2 0.0 reduce-scatter.5.cloned.1.call-update
  121.3 0.0 all-reduce.6.cloned.1.call-start
  121.3 0.3 multiply_reduce_fusion.5
  121.7 0.0 copy-done.4
  121.7 0.3 multiply_reduce_fusion.3
  122.0 19.4 %reduce-scatter.3.cloned.1.call-done = f32[16,512]{1,0:T(8,128)} async-done(((f32[64,512]{1,0:T(8,128)}), f32[16,512]{1,0:T(8,128)}) %reduce-scatter.3.cloned.1.call-update) | async-done | bytes 32784 | tf_op jit(solution)/shard_map/reduce_scatter | solution.py:80
  141.4 0.9 multiply_reduce_fusion.4
  142.4 2.8 convolution_bitcast_fusion
  145.2 29.6 %reduce-scatter.5.cloned.1.call-done = f32[16,512]{1,0:T(8,128)} async-done(((f32[128,512]{1,0:T(8,128)}), f32[16,512]{1,0:T(8,128)}) %reduce-scatter.5.cloned.1.call-update) | async-done | bytes 32784 | tf_op jit(solution)/shard_map/reduce_scatter | solution.py:81
  174.7 0.9 multiply_reduce_fusion.2
  175.7 2.4 convolution_bitcast_fusion.1
  178.1 0.0 all-reduce.6.cloned.1.call-update
  178.1 0.7 subtract_reduce_fusion.1
  180.7 0.6 subtract_reduce_fusion
  182.0 38.1 %psum.53 = f32[]{:T(128)} all-reduce(f32[]{:T(128)S(6)} %add.100), channel_id=1, replica_groups=mesh['img'=8,'txt'=4] {'img','txt'}, use_global_device_ids=true, to_apply=%region_24.0 | all-reduce | flops 1 | bytes 8 | tf_op jit(solution)/shard_map/psum | solution.py:84
  220.7 94.9 %all-reduce.6.cloned.1.call-done = (f32[768,512]{0,1:T(8,128)}, f32[512,512]{0,1:T(8,128)}) async-done(((f32[768,512]{0,1:T(8,128)}, f32[512,512]{0,1:T(8,128)}), (f32[768,512]{0,1:T(8,128)}, f32[512,512]{0,1:T(8,128)})) %all-reduce.6.cloned.1.call-update) | async-done | bytes 2621456 | tf_op jit(solution)/shard_map/psum | solution.py:84
  315.6 3.1 copy.9
  318.7 1.3 copy.10
  (10 shorter events, 0.0 us)
Async XLA Ops:
  7.2 21.9 %copy-start = (bf16[768,512]{1,0:T(8,128)(2,1)S(1)}, bf16[768,512]{1,0:T(8,128)(2,1)}, u32[]{:S(2)}) copy-start(bf16[768,512]{1,0:T(8,128)(2,1)} %param.10) | copy-start | bytes 2359300
  7.2 36.7 %copy-start.1 = (bf16[512,512]{1,0:T(8,128)(2,1)S(1)}, bf16[512,512]{1,0:T(8,128)(2,1)}, u32[]{:S(2)}) copy-start(bf16[512,512]{1,0:T(8,128)(2,1)} %param.11) | copy-start | bytes 1572868
  7.2 134.2 %reduce-scatter.3.cloned.1.call-start = ((), (), s32[]{:S(2)}) async-start(), calls=%async_computation.2 | async-start | bytes 163840 | tf_op jit(solution)/shard_map/reduce_scatter | solution.py:80
  44.2 77.1 %copy-start.3 = (bf16[16,768]{1,0:T(8,128)(2,1)S(1)}, bf16[16,768]{1,0:T(8,128)(2,1)}, u32[]{:S(2)}) copy-start(bf16[16,768]{1,0:T(8,128)(2,1)} %param.6) | copy-start | bytes 73732
  58.7 63.0 %copy-start.4 = (bf16[16,512]{1,0:T(8,128)(2,1)S(1)}, bf16[16,512]{1,0:T(8,128)(2,1)}, u32[]{:S(2)}) copy-start(bf16[16,512]{1,0:T(8,128)(2,1)} %param.7) | copy-start | bytes 49156
  120.2 54.5 %reduce-scatter.5.cloned.1.call-start = ((), (), s32[]{:S(2)}) async-start(), calls=%async_computation.3 | async-start | bytes 294912 | tf_op jit(solution)/shard_map/reduce_scatter | solution.py:81
  121.3 194.3 %all-reduce.6.cloned.1.call-start = ((), (), s32[]{:S(2)}) async-start(), calls=%async_computation.4 | async-start | bytes 5242880 | tf_op jit(solution)/shard_map/psum | solution.py:84
  315.6 3.1 copy-start.2
Sparse Core Ops, SparseCore 0:
  120.3 21.0 reduce-scatter.2
  144.3 30.3 reduce-scatter.4
  180.8 134.6 all-reduce.5
where the time goes:
time: 329 us; the launch traced here: 328 us
  blocking collectives  144 us (44%)
  waiting for transfers between devices  144 us (44%)
  between operations  18.2 us (6%)
  matrix products  9.06 us (3%)
  other arithmetic  7.8 us (2%)
  local copies, waits for them, and re-layouts  4.45 us (1%)
    psum x1, waiting for transfers between devices, shards(): lax.psum((local_img, local_txt, local_term), ('img', 'txt'))  94.9 us
    psum x1, blocking collectives, shards(): lax.psum((local_img, local_txt, local_term), ('img', 'txt'))  38.1 us
    reduce_scatter x1, waiting for transfers between devices, shards(): d_txt = lax.psum_scatter(part_txt, 'img', scatter_dimension=0, tiled=True)  29.6 us
    psum x2, blocking collectives, tile_terms(): lax.psum((jnp.sum(jnp.exp(tl - ctm[None, :]), 0), jnp.sum(jnp.exp(sl - cs...  27.2 us
    reduce_scatter x1, waiting for transfers between devices, shards(): d_img = lax.psum_scatter(part_img, 'txt', scatter_dimension=0, tiled=True)  19.4 us
    pmax x1, blocking collectives, tile_terms(): ctm, csm = lax.pmax((tl.max(0), sl.max(0)), 'img')  14.9 us
    all_gather x1, blocking collectives, shards(): lax.all_gather(text_feats, 'img', axis=0, tiled=True)  14.5 us
    all_gather x1, blocking collectives, shards(): lax.all_gather(q_txt, 'img', axis=0, tiled=True)  14.2 us
  transfers between devices with their start and end apart: 3, of which 3 were waited for; matrix products, arithmetic and copies ran while one was open for 2% of the time, Pallas kernels for 0%

commit v1 on v0

--- a/solution.py
+++ b/solution.py
@@ -1,6 +1,10 @@
+import functools
+
 import jax
 import jax.numpy as jnp
 from jax import lax
+from jax.experimental import pallas as pl
+from jax.experimental.pallas import tpu as pltpu
 from jax.sharding import PartitionSpec as P
 
 EPS = 1e-06
@@ -87,9 +91,267 @@
     return (loss, grad_img, grad_txt)
 
 
+MESH = pl.DeviceIdType.MESH
+FUSED_VMEM_BYTES = 44 * 1024 * 1024
+
+
+def dot_nt(a, b):
+    return lax.dot_general(a, b, (((1,), (1,)), ((), ())), preferred_element_type=jnp.float32)
+
+
+def dot_tn(a, b):
+    return lax.dot_general(a, b, (((0,), (0,)), ((), ())), preferred_element_type=jnp.float32)
+
+
+def gather_kernel(n_img, n_txt, image, text, t_img, t_txt, buf, sz, rz, sx, rx, sy, ry, sc, rc, sd, rd, scd, rcd):
+    img, txt = lax.axis_index("img"), lax.axis_index("txt")
+    nz = n_img // 2
+    core = lax.rem(img, 2)
+    other = img + 1 - 2 * core
+    x_txt = txt + 1 - 2 * lax.rem(txt, 2)
+    y_txt = lax.rem(txt + 2, 4)
+    d_txt = lax.rem(x_txt + 2, 4)
+
+    def source(k):
+        return lax.rem(img + n_img - 2 * k, n_img)
+
+    def slot(i, t):
+        return t * n_img + i
+
+    z_peers = [(lax.rem(img + 2 * k, n_img), txt) for k in range(1, nz)]
+    peers = z_peers + [(img, x_txt), (img, y_txt), (other, txt)]
+    barrier = pltpu.get_barrier_semaphore()
+    for peer in peers:
+        pl.semaphore_signal(barrier, inc=1, device_id=peer, device_id_type=MESH)
+
+    ft, fi, dt = text.shape[1], image.shape[1], t_img.shape[1]
+    half = buf.shape[3]
+    split = half - dt - ft
+    mine = slot(img, txt)
+    buf[mine, 0, :, 0:dt] = t_img[...]
+    buf[mine, 0, :, dt : dt + ft] = text[...]
+    buf[mine, 0, :, dt + ft : half] = image[:, 0:split]
+    buf[mine, 1, :, 0:dt] = t_txt[...]
+    buf[mine, 1, :, dt:half] = image[:, split:fi]
+    pl.semaphore_wait(barrier, len(peers))
+
+    started = []
+
+    def send(at, part, peer, ssem, rsem):
+        ref = buf.at[at] if part is None else buf.at[at, part]
+        copy = pltpu.make_async_remote_copy(
+            src_ref=ref, dst_ref=ref, send_sem=ssem, recv_sem=rsem, device_id=peer, device_id_type=MESH
+        )
+        copy.start()
+        started.append(copy)
+
+    def arrived(at, part, ssem, rsem):
+        ref = buf.at[at] if part is None else buf.at[at, part]
+        pltpu.make_async_remote_copy(
+            src_ref=ref, dst_ref=ref, send_sem=ssem, recv_sem=rsem, device_id=(other, txt), device_id_type=MESH
+        ).wait_recv()
+
+    def line_block(k):
+        at = slot(source(k), txt)
+        send(at, None, (img, x_txt), sx.at[k], rx.at[k])
+        send(at, None, (img, y_txt), sy.at[k], ry.at[k])
+        send(at, None, (other, txt), sc.at[0, k], rc.at[0, k])
+
+    for k in range(1, nz):
+        send(mine, None, z_peers[k - 1], sz.at[k - 1], rz.at[k - 1])
+    line_block(0)
+    for k in range(nz):
+        if k + 1 < nz:
+            arrived(slot(source(k + 1), txt), None, sz.at[k], rz.at[k])
+            line_block(k + 1)
+        from_x = slot(source(k), x_txt)
+        arrived(from_x, None, sx.at[k], rx.at[k])
+        send(from_x, 0, (img, y_txt), sd.at[0, k], rd.at[0, k])
+        send(from_x, None, (other, txt), sc.at[1, k], rc.at[1, k])
+        from_y = slot(source(k), y_txt)
+        arrived(from_y, None, sy.at[k], ry.at[k])
+        send(from_y, 1, (img, x_txt), sd.at[1, k], rd.at[1, k])
+        send(from_y, None, (other, txt), sc.at[2, k], rc.at[2, k])
+    for k in range(nz):
+        diagonal = slot(source(k), d_txt)
+        for part in range(2):
+            arrived(diagonal, part, sd.at[part, k], rd.at[part, k])
+            send(diagonal, part, (other, txt), scd.at[part, k], rcd.at[part, k])
+
+    other_source = lambda k: lax.rem(other + n_img - 2 * k, n_img)
+    for k in range(nz):
+        arrived(slot(other_source(k), txt), None, sc.at[0, k], rc.at[0, k])
+        arrived(slot(other_source(k), x_txt), None, sc.at[1, k], rc.at[1, k])
+        arrived(slot(other_source(k), y_txt), None, sc.at[2, k], rc.at[2, k])
+        for part in range(2):
+            arrived(slot(other_source(k), d_txt), part, scd.at[part, k], rcd.at[part, k])
+    for copy in started:
+        copy.wait_send()
+
+
+def gather_all(n_img, n_txt, image, text, t_img, t_txt):
+    rows = image.shape[0]
+    half = (image.shape[1] + text.shape[1] + 2 * t_img.shape[1]) // 2
+    nz = n_img // 2
+    dma = pltpu.SemaphoreType.DMA
+    vmem = pl.BlockSpec(memory_space=pltpu.VMEM)
+    pairs = [(nz - 1,), (nz,), (nz,), (3, nz), (2, nz), (2, nz)]
+    return pl.pallas_call(
+        functools.partial(gather_kernel, n_img, n_txt),
+        out_shape=jax.ShapeDtypeStruct((n_img * n_txt, 2, rows, half), image.dtype),
+        in_specs=[vmem] * 4,
+        out_specs=vmem,
+        scratch_shapes=[dma(shape) for shape in pairs for _ in range(2)],
+        compiler_params=pltpu.CompilerParams(
+            collective_id=0, has_side_effects=True, vmem_limit_bytes=FUSED_VMEM_BYTES
+        ),
+        name="gather_blocks",
+    )(image, text, t_img, t_txt)
+
+
+def loss_kernel(
+    buf, w_img, w_txt, loss, grad_img, grad_txt, f_img, e_img, e_txt, s_img, s_txt, q_img, q_txt, i_img, i_txt, tl, sl, ec_t, ec_s, g
+):
+    slots, _, rows, half = buf.shape
+    batch = slots * rows
+    fi, ds = w_img.shape
+    ft = w_txt.shape[0]
+    dt = q_img.shape[1]
+    chunk = 128
+    per = chunk // rows
+    steps = batch // chunk
+
+    def read(c, part, lo, hi):
+        return buf[pl.ds(c * per, per), part, :, lo:hi].reshape(chunk, hi - lo)
+
+    def embed(c, _):
+        at = pl.ds(pl.multiple_of(c * chunk, chunk), chunk)
+        q_img[at, :] = normed(read(c, 0, 0, dt))
+        q_txt[at, :] = normed(read(c, 1, 0, dt))
+        feats = jnp.concatenate([read(c, 0, dt + ft, half), read(c, 1, dt, half)], axis=1)
+        f_img[at, :] = feats
+        e, inv = project(feats, w_img[...])
+        e_img[at, :], i_img[at, :] = e, inv
+        s_img[at, :] = e.astype(jnp.bfloat16)
+        e, inv = project(read(c, 0, dt, dt + ft), w_txt[...])
+        e_txt[at, :], i_txt[at, :] = e, inv
+        s_txt[at, :] = e.astype(jnp.bfloat16)
+        return 0
+
+    lax.fori_loop(0, steps, embed, 0)
+
+    def logits(c, maxima):
+        at = pl.ds(pl.multiple_of(c * chunk, chunk), chunk)
+        t = TEACHER_SCALE * dot_nt(q_img[at, :], q_txt[...])
+        s = STUDENT_SCALE * dot_nt(s_img[at, :], s_txt[...])
+        tl[at, :], sl[at, :] = t, s
+        return (
+            jnp.maximum(maxima[0], jnp.max(t, axis=0, keepdims=True)),
+            jnp.maximum(maxima[1], jnp.max(s, axis=0, keepdims=True)),
+        )
+
+    low = jnp.full((1, batch), -jnp.inf, jnp.float32)
+    ctm, csm = lax.fori_loop(0, steps, logits, (low, low))
+
+    def row_terms(c, carry):
+        cts, css, terms, lse = carry
+        at = pl.ds(pl.multiple_of(c * chunk, chunk), chunk)
+        t, s = tl[at, :], sl[at, :]
+        rtm, rsm = jnp.max(t, axis=1, keepdims=True), jnp.max(s, axis=1, keepdims=True)
+        et, es = jnp.exp(t - rtm), jnp.exp(s - rsm)
+        rts, rss = jnp.sum(et, axis=1, keepdims=True), jnp.sum(es, axis=1, keepdims=True)
+        p = et * (1.0 / rts)
+        diff = t - s
+        ct, cs = jnp.exp(t - ctm), jnp.exp(s - csm)
+        ec_t[at, :], ec_s[at, :] = ct, cs
+        tl[at, :], sl[at, :] = diff, es * (1.0 / rss) - p
+        lse = lse + jnp.sum(rsm - rtm + jnp.log(rss) - jnp.log(rts), axis=0, keepdims=True)
+        terms = terms + jnp.sum(p * diff, axis=0, keepdims=True)
+        return (cts + jnp.sum(ct, axis=0, keepdims=True), css + jnp.sum(cs, axis=0, keepdims=True), terms, lse)
+
+    zero = jnp.zeros((1, batch), jnp.float32)
+    cts, css, terms, lse = lax.fori_loop(0, steps, row_terms, (zero, zero, zero, jnp.zeros((1, 1), jnp.float32)))
+    rct, rcs = 1.0 / cts, 1.0 / css
+    terms = terms + (csm - ctm + jnp.log(css) - jnp.log(cts))
+
+    def columns(c, terms):
+        at = pl.ds(pl.multiple_of(c * chunk, chunk), chunk)
+        p = ec_t[at, :] * rct
+        tile = 0.5 * STUDENT_SCALE * (sl[at, :] + (ec_s[at, :] * rcs - p))
+        g[at, :] = tile.astype(jnp.bfloat16)
+        return terms + jnp.sum(p * tl[at, :], axis=0, keepdims=True)
+
+    terms = lax.fori_loop(0, steps, columns, terms)
+    loss[...] = (jnp.sum(terms, axis=1, keepdims=True) + lse) / (2.0 * batch)
+
+    d_img = jnp.dot(g[...], s_txt[...], preferred_element_type=jnp.float32)
+    du = tangent(d_img, e_img[...], i_img[...]).astype(jnp.bfloat16)
+    grad_img[...] = dot_tn(f_img[...], du)
+    d_txt = dot_tn(g[...], s_img[...])
+    du = tangent(d_txt, e_txt[...], i_txt[...]).astype(jnp.bfloat16)
+    grad_txt[...] = dot_tn(buf[:, 0, :, dt : dt + ft].reshape(batch, ft), du)
+
+
+def loss_and_grads(gathered, w_img, w_txt, dt):
+    slots, _, rows, half = gathered.shape
+    batch = slots * rows
+    (fi, ds), ft = w_img.shape, w_txt.shape[0]
+    vmem = pl.BlockSpec(memory_space=pltpu.VMEM)
+    f32, b16 = jnp.float32, jnp.bfloat16
+    scratch = [
+        ((batch, fi), b16),
+        ((batch, ds), f32),
+        ((batch, ds), f32),
+        ((batch, ds), b16),
+        ((batch, ds), b16),
+        ((batch, dt), b16),
+        ((batch, dt), b16),
+        ((batch, 1), f32),
+        ((batch, 1), f32),
+    ]
+    scratch += [((batch, batch), f32)] * 4 + [((batch, batch), b16)]
+    return pl.pallas_call(
+        loss_kernel,
+        out_shape=[
+            jax.ShapeDtypeStruct((1, 1), f32),
+            jax.ShapeDtypeStruct((fi, ds), f32),
+            jax.ShapeDtypeStruct((ft, ds), f32),
+        ],
+        in_specs=[vmem] * 3,
+        out_specs=[vmem] * 3,
+        scratch_shapes=[pltpu.VMEM(*s) for s in scratch],
+        compiler_params=pltpu.CompilerParams(vmem_limit_bytes=FUSED_VMEM_BYTES),
+        name="loss_and_grads",
+    )(gathered, w_img, w_txt)
+
+
+def whole_batch(n_img, n_txt, image_feats, text_feats, teacher_img, teacher_txt, proj_img, proj_txt):
+    gathered = gather_all(n_img, n_txt, image_feats, text_feats, teacher_img, teacher_txt)
+    loss, grad_img, grad_txt = loss_and_grads(gathered, proj_img, proj_txt, teacher_img.shape[1])
+    return (loss.reshape(()), grad_img, grad_txt)
+
+
+def fits(n_img, n_txt, image, text, t_img, t_txt, proj_img, proj_txt):
+    rows, fi = image.shape
+    batch = rows * n_img * n_txt
+    ft, dt, ds = text.shape[1], t_img.shape[1], proj_img.shape[1]
+    columns = fi + ft + 2 * dt
+    split = columns // 2 - dt - ft
+    held = 2 * batch * (2 * columns + fi) + 12 * batch * ds + 18 * batch * batch + 6 * ds * (fi + ft)
+    aligned = rows % 16 == 0 and 128 % rows == 0 and batch % 128 == 0 and split > 0 and split % 128 == 0 and columns % 256 == 0
+    return n_txt == 4 and n_img % 2 == 0 and n_img > 2 and aligned and held <= FUSED_VMEM_BYTES * 3 // 4
+
+
 def solution(mesh):
+    n_img, n_txt = mesh.shape["img"], mesh.shape["txt"]
+
+    def per_device(*arrays):
+        if fits(n_img, n_txt, *arrays):
+            return whole_batch(n_img, n_txt, *arrays)
+        return shards(*arrays)
+
     return jax.shard_map(
-        shards,
+        per_device,
         mesh=mesh,
         in_specs=(
             P(("img", "txt"), None),

time: 329 us -> 40.1 us (0.12)
  blocking collectives: 144 us -> 0 us
  waiting for transfers between devices: 144 us -> 0 us
  Pallas kernels: 0 us -> 36 us
  between operations: 18.2 us -> 0.68 us
  matrix products: 9.06 us -> 0 us
  other arithmetic: 7.8 us -> 0 us
    psum x1 -> x0, waiting for transfers between devices: 94.9 us -> none  [shards(): lax.psum((local_img, local_txt, local_term), ('img', 'txt'))]
    psum x4 -> x0, blocking collectives: 73.4 us -> none  [the longest x1 38.1 us: shards(): lax.psum((local_img, local_txt, local_term), ('img', 'txt'))]
    reduce_scatter x2 -> x0, waiting for transfers between devices: 49 us -> none  [the longest x1 29.6 us: shards(): d_txt = lax.psum_scatter(part_txt, 'img', scatter_dimension=0, tiled=True)]
    all_gather x4 -> x0, blocking collectives: 46.9 us -> none  [the longest x1 14.5 us: shards(): lax.all_gather(text_feats, 'img', axis=0, tiled=True)]
    pallas_call x0 -> x2, Pallas kernels: none -> 36 us  [the longest x1 27 us: gather_all(): pl.pallas_call(functools.partial(gather_kernel, n_img, n_txt), out_shape=...]
    pmax x2 -> x0, blocking collectives: 23.8 us -> none  [the longest x1 14.9 us: tile_terms(): ctm, csm = lax.pmax((tl.max(0), sl.max(0)), 'img')]
    dot_general x10 -> x0, matrix products: 9.06 us -> none  [the longest x2 5.23 us: weight_grad(): lax.dot_general(feats.astype(jnp.float32), du_rows, (((0,), (0,)), ((), (...]
    reduce_sum x8 -> x0, other arithmetic: 5.91 us -> none  [the longest x2 1.88 us: tangent(): jnp.sum(embeds * grad_rows, 1, keepdims=True)]
  transfers between devices with their start and end apart: 3 -> 0, of which waited for: 3 -> 0; matrix products, arithmetic and copies ran while one was open for 2% -> 0% of each run, Pallas kernels for 0% -> 0%
where the time goes in v1:
time: 40.1 us; the launch traced here: 39.8 us
  Pallas kernels  36 us (90%)
  local copies, waits for them, and re-layouts  3.07 us (8%)
  between operations  0.68 us (2%)
    pallas_call x1, Pallas kernels, gather_all(): pl.pallas_call(functools.partial(gather_kernel, n_img, n_txt), out_shape=...  27 us
    pallas_call x1, Pallas kernels, loss_and_grads(): pl.pallas_call(loss_kernel, out_shape=[jax.ShapeDtypeStruct((1, 1), f32),...  9.09 us
    unnamed x12, local copies, waits for them, and re-layouts  3.07 us

profile of v1, /device:TPU:0, one launch (start us, length us, event | category | flops | bytes accessed | tf_op | source)
XLA Modules:
  0.0 39.8 jit_solution(14072548868082902602)
XLA Ops:
  0.6 0.0 copy-start.1
  0.6 0.0 copy-start
  0.7 0.0 copy-start.2
  0.7 0.8 %copy-done.2 = bf16[16,1024]{1,0:T(8,128)(2,1)S(1)} copy-done((bf16[16,1024]{1,0:T(8,128)(2,1)S(1)}, bf16[16,1024]{1,0:T(8,128)(2,1)}, u32[]{:S(2)}) %copy-start.2) | copy-done | bytes 32792
  1.5 0.0 copy-start.3
  1.5 0.8 %copy-done.3 = bf16[16,1024]{1,0:T(8,128)(2,1)S(1)} copy-done((bf16[16,1024]{1,0:T(8,128)(2,1)S(1)}, bf16[16,1024]{1,0:T(8,128)(2,1)}, u32[]{:S(2)}) %copy-start.3) | copy-done | bytes 32792
  2.3 0.0 copy-start.4
  2.3 0.7 %copy-done.4 = bf16[16,768]{1,0:T(8,128)(2,1)S(1)} copy-done((bf16[16,768]{1,0:T(8,128)(2,1)S(1)}, bf16[16,768]{1,0:T(8,128)(2,1)}, u32[]{:S(2)}) %copy-start.4) | copy-done | bytes 24600
  3.0 0.0 copy-start.5
  3.0 0.7 %copy-done.5 = bf16[16,512]{1,0:T(8,128)(2,1)S(1)} copy-done((bf16[16,512]{1,0:T(8,128)(2,1)S(1)}, bf16[16,512]{1,0:T(8,128)(2,1)}, u32[]{:S(2)}) %copy-start.5) | copy-done | bytes 16408
  3.7 27.0 %gather_blocks.1.buf = bf16[32,2,16,1664]{3,2,1,0:T(8,128)(2,1)S(1)} custom-call(bf16[16,768]{1,0:T(8,128)(2,1)S(1)} %copy-done.4, bf16[16,512]{1,0:T(8,128)(2,1)S(1)} %copy-done.5, bf16[16,1024]{1,0:T(8,128)(2,1)S(1)} %copy-done.2, bf16[16,1024]{1,0:T(8,128)(2,1)S(1)} %copy-done.3), custom_call_target="tpu_custom_call" | custom-call | tf_op jit(solution)/shard_map/gather_blocks/pallas_call | solution.py:199
  30.7 0.0 copy-done.1
  30.7 0.0 copy-done
  30.7 9.1 %loss_and_grads.1 = (f32[1,1]{1,0:T(1,128)}, f32[768,512]{1,0:T(8,128)}, f32[512,512]{1,0:T(8,128)}) custom-call(bf16[32,2,16,1664]{3,2,1,0:T(8,128)(2,1)S(1)} %gather_blocks.1.buf, bf16[768,512]{1,0:T(8,128)(2,1)S(1)} %copy-done, bf16[512,512]{1,0:T(8,128)(2,1)S(1)} %copy-done.1), custom_call_target="tpu_custom_call" | custom-call | tf_op jit(solution)/shard_map/loss_and_grads/pallas_call | solution.py:313
Async XLA Ops:
  0.6 30.1 %copy-start.1 = (bf16[512,512]{1,0:T(8,128)(2,1)S(1)}, bf16[512,512]{1,0:T(8,128)(2,1)}, u32[]{:S(2)}) copy-start(bf16[512,512]{1,0:T(8,128)(2,1)} %w_txt.1) | copy-start | bytes 1572868
  0.6 30.1 %copy-start = (bf16[768,512]{1,0:T(8,128)(2,1)S(1)}, bf16[768,512]{1,0:T(8,128)(2,1)}, u32[]{:S(2)}) copy-start(bf16[768,512]{1,0:T(8,128)(2,1)} %w_img.1) | copy-start | bytes 2359300
  0.7 0.9 %copy-start.2 = (bf16[16,1024]{1,0:T(8,128)(2,1)S(1)}, bf16[16,1024]{1,0:T(8,128)(2,1)}, u32[]{:S(2)}) copy-start(bf16[16,1024]{1,0:T(8,128)(2,1)} %t_img.1) | copy-start | bytes 98308
  1.5 0.8 %copy-start.3 = (bf16[16,1024]{1,0:T(8,128)(2,1)S(1)}, bf16[16,1024]{1,0:T(8,128)(2,1)}, u32[]{:S(2)}) copy-start(bf16[16,1024]{1,0:T(8,128)(2,1)} %t_txt.1) | copy-start | bytes 98308
  2.3 0.7 %copy-start.4 = (bf16[16,768]{1,0:T(8,128)(2,1)S(1)}, bf16[16,768]{1,0:T(8,128)(2,1)}, u32[]{:S(2)}) copy-start(bf16[16,768]{1,0:T(8,128)(2,1)} %image.1) | copy-start | bytes 73732
  3.0 0.7 %copy-start.5 = (bf16[16,512]{1,0:T(8,128)(2,1)S(1)}, bf16[16,512]{1,0:T(8,128)(2,1)}, u32[]{:S(2)}) copy-start(bf16[16,512]{1,0:T(8,128)(2,1)} %text.1) | copy-start | bytes 49156

commit v2 on v0

--- a/solution.py
+++ b/solution.py
@@ -1,6 +1,10 @@
+import functools
+
 import jax
 import jax.numpy as jnp
 from jax import lax
+from jax.experimental import pallas as pl
+from jax.experimental.pallas import tpu as pltpu
 from jax.sharding import PartitionSpec as P
 
 EPS = 1e-06
@@ -87,9 +91,449 @@
     return (loss, grad_img, grad_txt)
 
 
+MESH = pl.DeviceIdType.MESH
+FUSED_VMEM_BYTES = 60 * 1024 * 1024
+LANES = 128
+
+
+def dot_nt(a, b):
+    return lax.dot_general(a, b, (((1,), (1,)), ((), ())), preferred_element_type=jnp.float32)
+
+
+def dot_tn(a, b):
+    return lax.dot_general(a, b, (((0,), (0,)), ((), ())), preferred_element_type=jnp.float32)
+
+
+class Spread:
+    def __init__(self, place, buf, halves, sems, log):
+        self.place, self.buf, self.halves, self.log = place, buf, halves, log
+        self.sz, self.rz, self.sx, self.rx, self.sy, self.ry, self.sc, self.rc, self.sd, self.rd, self.se, self.re = sems
+
+    def ref(self, at, part):
+        if part is None:
+            return self.buf.at[at]
+        lo, hi = self.halves[part]
+        return self.buf.at[at, lo:hi]
+
+    def copy(self, at, part, peer, ssem, rsem):
+        ref = self.ref(at, part)
+        return pltpu.make_async_remote_copy(
+            src_ref=ref, dst_ref=ref, send_sem=ssem, recv_sem=rsem, device_id=peer, device_id_type=MESH
+        )
+
+    def send(self, *args):
+        copy = self.copy(*args)
+        copy.start()
+        self.log.append(copy)
+
+    def arrived(self, at, part, ssem, rsem):
+        self.copy(at, part, self.place.partner, ssem, rsem).wait_recv()
+
+    def own(self):
+        p = self.place
+        for k in range(1, p.nz):
+            self.send(p.slot(p.img, p.txt), None, p.z_peer(k), self.sz.at[k - 1], self.rz.at[k - 1])
+        self.line(0)
+
+    def line(self, k):
+        p = self.place
+        at = p.slot(p.source(k), p.txt)
+        if k > 0:
+            self.arrived(at, None, self.sz.at[k - 1], self.rz.at[k - 1])
+        self.send(at, None, (p.img, p.x_txt), self.sx.at[k], self.rx.at[k])
+        self.send(at, None, (p.img, p.y_txt), self.sy.at[k], self.ry.at[k])
+        self.send(at, None, p.partner, self.sc.at[0, k], self.rc.at[0, k])
+
+    def turn(self, k):
+        p = self.place
+        at = p.slot(p.source(k), p.x_txt)
+        self.arrived(at, None, self.sx.at[k], self.rx.at[k])
+        self.send(at, 0, (p.img, p.y_txt), self.sd.at[0, k], self.rd.at[0, k])
+        self.send(at, None, p.partner, self.sc.at[1, k], self.rc.at[1, k])
+        at = p.slot(p.source(k), p.y_txt)
+        self.arrived(at, None, self.sy.at[k], self.ry.at[k])
+        self.send(at, 1, (p.img, p.x_txt), self.sd.at[1, k], self.rd.at[1, k])
+        self.send(at, None, p.partner, self.sc.at[2, k], self.rc.at[2, k])
+
+    def last(self, k):
+        p = self.place
+        at = p.slot(p.source(k), p.d_txt)
+        for part in range(2):
+            self.arrived(at, part, self.sd.at[part, k], self.rd.at[part, k])
+            self.send(at, part, p.partner, self.se.at[part, k], self.re.at[part, k])
+
+    def whole(self, which):
+        p = self.place
+        for k in range(p.nz):
+            source = p.other_source(k)
+            if which < 3:
+                at = p.slot(source, (p.txt, p.x_txt, p.y_txt)[which])
+                self.arrived(at, None, self.sc.at[which, k], self.rc.at[which, k])
+            else:
+                for part in range(2):
+                    self.arrived(p.slot(source, p.d_txt), part, self.se.at[part, k], self.re.at[part, k])
+
+
+class Place:
+    def __init__(self, n_img, n_txt):
+        self.n_img, self.n_txt, self.nz = n_img, n_txt, n_img // 2
+        self.img, self.txt = lax.axis_index("img"), lax.axis_index("txt")
+        self.other = self.img + 1 - 2 * lax.rem(self.img, 2)
+        self.partner = (self.other, self.txt)
+        self.x_txt = self.txt + 1 - 2 * lax.rem(self.txt, 2)
+        self.y_txt = lax.rem(self.txt + 2, 4)
+        self.d_txt = lax.rem(self.x_txt + 2, 4)
+
+    def slot(self, img, txt):
+        return txt * self.n_img + img
+
+    def source(self, k):
+        return lax.rem(self.img + self.n_img - 2 * k, self.n_img)
+
+    def other_source(self, k):
+        return lax.rem(self.other + self.n_img - 2 * k, self.n_img)
+
+    def z_peer(self, k):
+        return (lax.rem(self.img + 2 * k, self.n_img), self.txt)
+
+    def img_at(self, k):
+        return lax.rem(self.img + k, self.n_img)
+
+    def txt_at(self, k):
+        return lax.rem(self.txt + k, self.n_txt)
+
+
+def exchange_kernel(n_img, n_txt, image, text, t_img, t_txt, p_img, p_txt, *refs):
+    loss, feats_out, du_img_out, du_txt_out = refs[:4]
+    feats, tiles, e_img, e_txt, i_img, i_txt, s_img, s_txt, sl, ps, du_img, du_txt = refs[4:16]
+    raw, q_img, q_txt, tile, row_st, col_st, w_img, w_txt, g_tile, load = refs[16:26]
+    tz_s, tz_r, tc_s, tc_r, ti_s, ti_r, rs_s, rs_r, cs_s, cs_r = refs[26:36]
+    f_sems, p_sems = refs[36:48], refs[48:60]
+    p = Place(n_img, n_txt)
+    nz, img, txt = p.nz, p.img, p.txt
+    rows, fi = image.shape
+    ft, dt = text.shape[1], t_img.shape[1]
+    half = feats.shape[3]
+    batch = sl.shape[0]
+    mine = p.slot(img, txt)
+
+    loads = [
+        pltpu.make_async_copy(t_img, raw.at[0], load.at[0]),
+        pltpu.make_async_copy(t_txt, raw.at[1], load.at[1]),
+        pltpu.make_async_copy(image.at[:, 0:half], feats.at[mine, 0], load.at[2]),
+        pltpu.make_async_copy(image.at[:, half:fi], feats.at[mine, 1, :, 0 : fi - half], load.at[3]),
+        pltpu.make_async_copy(text, feats.at[mine, 1, :, fi - half : half], load.at[4]),
+        pltpu.make_async_copy(p_img, w_img, load.at[5]),
+        pltpu.make_async_copy(p_txt, w_txt, load.at[6]),
+    ]
+    for copy in loads:
+        copy.start()
+    peers = [(p.img_at(k), txt) for k in range(1, n_img)] + [(img, p.txt_at(k)) for k in range(1, n_txt)]
+    barrier = pltpu.get_barrier_semaphore()
+    for peer in peers:
+        pl.semaphore_signal(barrier, inc=1, device_id=peer, device_id_type=MESH)
+    loads[0].wait()
+    q_img[txt] = normed(raw[0])
+    loads[1].wait()
+    q_txt[img] = normed(raw[1])
+    for copy in loads[2:5]:
+        copy.wait()
+    pl.semaphore_wait(barrier, len(peers))
+
+    log = []
+
+    def copy_of(ref, peer, ssem, rsem):
+        return pltpu.make_async_remote_copy(
+            src_ref=ref, dst_ref=ref, send_sem=ssem, recv_sem=rsem, device_id=peer, device_id_type=MESH
+        )
+
+    def send(*args):
+        copy = copy_of(*args)
+        copy.start()
+        log.append(copy)
+
+    def arrived(ref, ssem, rsem):
+        copy_of(ref, p.partner, ssem, rsem).wait_recv()
+
+    f = Spread(p, feats, ((0, 1), (1, 2)), f_sems, log)
+    rows_in, cols_in = rows * n_txt, rows * n_img
+    g = Spread(p, tiles, ((0, rows_in // 2), (rows_in // 2, rows_in + 16)), p_sems, log)
+
+    for k in range(1, nz):
+        send(q_txt.at[img], p.z_peer(k), tz_s.at[k - 1], tz_r.at[k - 1])
+    for k in range(1, n_txt):
+        send(q_img.at[txt], (img, p.txt_at(k)), ti_s.at[k - 1], ti_r.at[k - 1])
+    send(q_txt.at[img], p.partner, tc_s.at[0], tc_r.at[0])
+    f.own()
+    for k in range(1, nz):
+        arrived(q_txt.at[p.source(k)], tz_s.at[k - 1], tz_r.at[k - 1])
+        send(q_txt.at[p.source(k)], p.partner, tc_s.at[k], tc_r.at[k])
+    for k in range(1, n_txt):
+        arrived(q_img.at[p.txt_at(n_txt - k)], ti_s.at[k - 1], ti_r.at[k - 1])
+    for k in range(nz):
+        arrived(q_txt.at[p.other_source(k)], tc_s.at[k], tc_r.at[k])
+
+    t = TEACHER_SCALE * dot_nt(q_img[...].reshape(rows_in, dt), q_txt[...].reshape(cols_in, dt))
+    tile[...] = t
+    m = jnp.max(t, axis=1, keepdims=True)
+    s = jnp.sum(jnp.exp(t - m), axis=1, keepdims=True)
+    lane = lax.broadcasted_iota(jnp.int32, (rows_in, cols_in), 1)
+    packed = jnp.where(lane < rows_in, m, s).T
+    row_st[txt] = jnp.zeros(row_st.shape[1:], jnp.float32)
+    row_st[txt, 0:1, 0:rows_in] = packed[0:1, :]
+    row_st[txt, 1:2, 0:rows_in] = packed[rows_in : rows_in + 1, :]
+    m = jnp.max(t, axis=0, keepdims=True)
+    col_st[img] = jnp.zeros(col_st.shape[1:], jnp.float32)
+    col_st[img, 0:1, :] = m
+    col_st[img, 1:2, :] = jnp.sum(jnp.exp(t - m), axis=0, keepdims=True)
+    for k in range(1, n_img):
+        send(col_st.at[img], (p.img_at(k), txt), cs_s.at[k - 1], cs_r.at[k - 1])
+    for k in range(1, n_txt):
+        send(row_st.at[txt], (img, p.txt_at(k)), rs_s.at[k - 1], rs_r.at[k - 1])
+
+    for k in range(1, nz):
+        f.line(k)
+    for k in range(1, n_img):
+        arrived(col_st.at[p.img_at(n_img - k)], cs_s.at[k - 1], cs_r.at[k - 1])
+    for k in range(1, n_txt):
+        arrived(row_st.at[p.txt_at(n_txt - k)], rs_s.at[k - 1], rs_r.at[k - 1])
+
+    def log_sum(stats):
+        m = jnp.max(stats[:, 0, :], axis=0, keepdims=True)
+        return m + jnp.log(jnp.sum(stats[:, 1, :] * jnp.exp(stats[:, 0, :] - m), axis=0, keepdims=True))
+
+    lz_row = log_sum(row_st[:, :, 0:rows_in])
+    lz_col = log_sum(col_st[...])
+    t = tile[...]
+    both = jnp.exp(t - jnp.broadcast_to(lz_row, (cols_in, rows_in)).T) + jnp.exp(t - lz_col)
+    part = jnp.sum(both * t, axis=0, keepdims=True) - lz_col / n_img
+    part = part - jnp.sum(lz_row, axis=1, keepdims=True) / (n_txt * cols_in)
+    high = part.astype(jnp.bfloat16).astype(jnp.float32)
+    middle = (part - high).astype(jnp.bfloat16).astype(jnp.float32)
+    line = lax.broadcasted_iota(jnp.int32, (16, cols_in), 0)
+    pieces = jnp.where(line == 0, high, jnp.where(line == 1, middle, jnp.where(line == 2, part - high - middle, 0.0)))
+    tiles[mine, 0:rows_in, :] = both.astype(jnp.bfloat16)
+    tiles[mine, rows_in : rows_in + 16, :] = pieces.astype(jnp.bfloat16)
+    g.own()
+
+    def embed(j):
+        at = pl.ds(pl.multiple_of(j * cols_in, cols_in), cols_in)
+        here = pl.ds(j * n_img, n_img)
+        rest = feats[here, 1].reshape(cols_in, half)
+        x = jnp.concatenate([feats[here, 0].reshape(cols_in, half), rest[:, 0 : fi - half]], axis=1)
+        e, inv = project(x, w_img[...])
+        e_img[at, :], i_img[at, :] = e, inv
+        s_img[at, :] = e.astype(jnp.bfloat16)
+        e, inv = project(rest[:, fi - half : half], w_txt[...])
+        e_txt[at, :], i_txt[at, :] = e, inv
+        s_txt[at, :] = e.astype(jnp.bfloat16)
+
+    for k in range(nz):
+        f.turn(k)
+    f.whole(0)
+    for copy in loads[5:]:
+        copy.wait()
+    embed(txt)
+    for k in range(1, nz):
+        g.line(k)
+    for k in range(nz):
+        f.last(k)
+    f.whole(1)
+    embed(p.x_txt)
+    for k in range(nz):
+        g.turn(k)
+    f.whole(2)
+    embed(p.y_txt)
+    f.whole(3)
+    embed(p.d_txt)
+    outs = [pltpu.make_async_copy(feats, feats_out, load.at[0])]
+    outs[0].start()
+    for k in range(nz):
+        g.last(k)
+
+    def logits(c, carry):
+        csm, total = carry
+        at = pl.ds(pl.multiple_of(c * cols_in, cols_in), cols_in)
+        s = STUDENT_SCALE * dot_nt(s_img[at, :], s_txt[...])
+        sl[at, :] = s
+        m = jnp.max(s, axis=1, keepdims=True)
+        es = jnp.exp(s - m)
+        sums = jnp.sum(es, axis=1, keepdims=True)
+        ps[at, :] = es * (1.0 / sums)
+        total = total + jnp.sum(m + jnp.log(sums), axis=0, keepdims=True)
+        return jnp.maximum(csm, jnp.max(s, axis=0, keepdims=True)), total
+
+    low = jnp.full((1, batch), -jnp.inf, jnp.float32)
+    csm, total = lax.fori_loop(0, n_txt, logits, (low, jnp.zeros((1, 1), jnp.float32)))
+
+    def sums(c, css):
+        at = pl.ds(pl.multiple_of(c * cols_in, cols_in), cols_in)
+        return css + jnp.sum(jnp.exp(sl[at, :] - csm), axis=0, keepdims=True)
+
+    css = lax.fori_loop(0, n_txt, sums, jnp.zeros((1, batch), jnp.float32))
+    lzc = csm + jnp.log(css)
+    total = total + jnp.sum(lzc, axis=1, keepdims=True)
+    for which in range(4):
+        g.whole(which)
+
+    def tile_rows(c):
+        held = [tiles[i * n_img : (i + 1) * n_img, pl.ds(pl.multiple_of(c * rows, rows), rows), :] for i in range(n_txt)]
+        return jnp.concatenate([h.reshape(cols_in, cols_in) for h in held], axis=1).astype(jnp.float32)
+
+    def gradient(c, terms):
+        at = pl.ds(pl.multiple_of(c * cols_in, cols_in), cols_in)
+        pt, s = tile_rows(c), sl[at, :]
+        g_tile[at, :] = (0.5 * STUDENT_SCALE * (ps[at, :] + jnp.exp(s - lzc) - pt)).astype(jnp.bfloat16)
+        return terms - jnp.sum(pt * s, axis=0, keepdims=True)
+
+    terms = lax.fori_loop(0, n_txt, gradient, jnp.zeros((1, batch), jnp.float32))
+    d_img = jnp.dot(g_tile[...], s_txt[...], preferred_element_type=jnp.float32)
+    du_img[...] = tangent(d_img, e_img[...], i_img[...]).astype(jnp.bfloat16)
+    outs.append(pltpu.make_async_copy(du_img, du_img_out, load.at[1]))
+    outs[1].start()
+    d_txt = dot_tn(g_tile[...], s_img[...])
+    du_txt[...] = tangent(d_txt, e_txt[...], i_txt[...]).astype(jnp.bfloat16)
+    outs.append(pltpu.make_async_copy(du_txt, du_txt_out, load.at[2]))
+    outs[2].start()
+    parts = jnp.sum(tiles[:, rows_in : rows_in + 16, :].astype(jnp.float32), axis=0)
+    total = total + jnp.sum(terms, axis=1, keepdims=True)
+    total = total + jnp.sum(jnp.sum(parts, axis=0, keepdims=True), axis=1, keepdims=True)
+    loss[...] = total / (2.0 * batch)
+    for copy in log:
+        copy.wait_send()
+    for copy in outs:
+        copy.wait()
+
+
+def exchange(n_img, n_txt, image, text, t_img, t_txt, w_img, w_txt):
+    rows, fi = image.shape
+    ft, dt, ds = text.shape[1], t_img.shape[1], w_img.shape[1]
+    nz, slots = n_img // 2, n_img * n_txt
+    batch, rows_in, cols_in = rows * slots, rows * n_txt, rows * n_img
+    f32, b16 = jnp.float32, jnp.bfloat16
+    dma = pltpu.SemaphoreType.DMA
+    vmem = pl.BlockSpec(memory_space=pltpu.VMEM)
+    hbm = pl.BlockSpec(memory_space=pltpu.HBM)
+    outs = [((1, 1), f32), ((slots, 2, rows, (fi + ft) // 2), b16), ((batch, ds), b16), ((batch, ds), b16)]
+    held = [
+        ((slots, 2, rows, (fi + ft) // 2), b16),
+        ((slots, rows_in + 16, cols_in), b16),
+        ((batch, ds), f32),
+        ((batch, ds), f32),
+        ((batch, 1), f32),
+        ((batch, 1), f32),
+        ((batch, ds), b16),
+        ((batch, ds), b16),
+        ((batch, batch), f32),
+        ((batch, batch), f32),
+        ((batch, ds), b16),
+        ((batch, ds), b16),
+    ]
+    scratch = [pltpu.VMEM(*h) for h in held] + [
+        pltpu.VMEM((2, rows, dt), b16),
+        pltpu.VMEM((n_txt, rows, dt), b16),
+        pltpu.VMEM((n_img, rows, dt), b16),
+        pltpu.VMEM((rows_in, cols_in), f32),
+        pltpu.VMEM((n_txt, 8, LANES), f32),
+        pltpu.VMEM((n_img, 8, LANES), f32),
+        pltpu.VMEM((fi, ds), b16),
+        pltpu.VMEM((ft, ds), b16),
+        pltpu.VMEM((batch, batch), b16),
+        dma((7,)),
+    ]
+    spread = [(nz - 1,), (nz,), (nz,), (3, nz), (2, nz), (2, nz)]
+    for shape in [(nz - 1,), (nz,), (n_txt - 1,), (n_txt - 1,), (n_img - 1,)] + spread + spread:
+        scratch += [dma(shape), dma(shape)]
+    return pl.pallas_call(
+        functools.partial(exchange_kernel, n_img, n_txt),
+        out_shape=[jax.ShapeDtypeStruct(*s) for s in outs],
+        in_specs=[hbm] * 6,
+        out_specs=[vmem] + [hbm] * 3,
+        scratch_shapes=scratch,
+        compiler_params=pltpu.CompilerParams(
+            collective_id=0, has_side_effects=True, vmem_limit_bytes=FUSED_VMEM_BYTES
+        ),
+        name="exchange_and_embed",
+    )(image, text, t_img, t_txt, w_img, w_txt)
+
+
+def grads_kernel(loss_in, feats_in, du_img_in, du_txt_in, loss, grad_img, grad_txt, feats, du_img, du_txt, g_img, g_txt, load, store):
+    slots, _, rows, half = feats.shape
+    batch = slots * rows
+    fi = grad_img.shape[0]
+    loads = [
+        pltpu.make_async_copy(du_img_in, du_img, load.at[0]),
+        pltpu.make_async_copy(feats_in, feats, load.at[1]),
+        pltpu.make_async_copy(du_txt_in, du_txt, load.at[2]),
+    ]
+    for copy in loads:
+        copy.start()
+    loss[...] = loss_in[...]
+    for copy in loads[:2]:
+        copy.wait()
+    g_img[0:half, :] = dot_tn(feats[:, 0].reshape(batch, half), du_img[...])
+    first = pltpu.make_async_copy(g_img.at[0:half], grad_img.at[0:half], store.at[0])
+    first.start()
+    g_img[half:fi, :] = dot_tn(feats[:, 1, :, 0 : fi - half].reshape(batch, fi - half), du_img[...])
+    second = pltpu.make_async_copy(g_img.at[half:fi], grad_img.at[half:fi], store.at[1])
+    second.start()
+    loads[2].wait()
+    g_txt[...] = dot_tn(feats[:, 1, :, fi - half : half].reshape(batch, 2 * half - fi), du_txt[...])
+    third = pltpu.make_async_copy(g_txt, grad_txt, store.at[2])
+    third.start()
+    for copy in (first, second, third):
+        copy.wait()
+
+
+def whole_batch(n_img, n_txt, image_feats, text_feats, teacher_img, teacher_txt, proj_img, proj_txt):
+    held = exchange(n_img, n_txt, image_feats, text_feats, teacher_img, teacher_txt, proj_img, proj_txt)
+    (fi, ds), ft = proj_img.shape, proj_txt.shape[0]
+    vmem = pl.BlockSpec(memory_space=pltpu.VMEM)
+    hbm = pl.BlockSpec(memory_space=pltpu.HBM)
+    f32 = jnp.float32
+    loss, grad_img, grad_txt = pl.pallas_call(
+        grads_kernel,
+        out_shape=[
+            jax.ShapeDtypeStruct((1, 1), f32),
+            jax.ShapeDtypeStruct((fi, ds), f32),
+            jax.ShapeDtypeStruct((ft, ds), f32),
+        ],
+        in_specs=[vmem] + [hbm] * 3,
+        out_specs=[vmem] + [hbm] * 2,
+        scratch_shapes=[pltpu.VMEM(h.shape, h.dtype) for h in held[1:]]
+        + [
+            pltpu.VMEM((fi, ds), f32),
+            pltpu.VMEM((ft, ds), f32),
+            pltpu.SemaphoreType.DMA((3,)),
+            pltpu.SemaphoreType.DMA((3,)),
+        ],
+        compiler_params=pltpu.CompilerParams(vmem_limit_bytes=FUSED_VMEM_BYTES),
+        name="weight_grads",
+    )(*held)
+    return (loss.reshape(()), grad_img, grad_txt)
+
+
+def fits(n_img, n_txt, image, text, t_img, t_txt, proj_img, proj_txt):
+    rows, fi = image.shape
+    batch = rows * n_img * n_txt
+    ft, dt, ds = text.shape[1], t_img.shape[1], proj_img.shape[1]
+    half = (fi + ft) // 2
+    held = 2 * batch * (fi + ft) + 12 * batch * ds + 16 * batch * batch + 6 * ds * (fi + ft)
+    aligned = rows % 16 == 0 and rows * n_img == LANES and rows * n_txt * 2 <= LANES and ft % 128 == 0 and dt % 128 == 0
+    aligned = aligned and fi % 128 == 0 and (fi + ft) % 256 == 0 and half < fi and (rows * n_txt) % 32 == 0
+    return n_txt == 4 and n_img % 2 == 0 and n_img > 2 and aligned and held <= FUSED_VMEM_BYTES * 3 // 4
+
+
 def solution(mesh):
+    n_img, n_txt = mesh.shape["img"], mesh.shape["txt"]
+
+    def per_device(*arrays):
+        if fits(n_img, n_txt, *arrays):
+            return whole_batch(n_img, n_txt, *arrays)
+        return shards(*arrays)
+
     return jax.shard_map(
-        shards,
+        per_device,
         mesh=mesh,
         in_specs=(
             P(("img", "txt"), None),

time: 329 us -> 39 us (0.12)
  blocking collectives: 144 us -> 0 us
  waiting for transfers between devices: 144 us -> 0 us
  Pallas kernels: 0 us -> 38.2 us
  between operations: 18.2 us -> 0.64 us
  matrix products: 9.06 us -> 0 us
  other arithmetic: 7.8 us -> 0 us
  local copies, waits for them, and re-layouts: 4.45 us -> 0 us
    psum x1 -> x0, waiting for transfers between devices: 94.9 us -> none  [shards(): lax.psum((local_img, local_txt, local_term), ('img', 'txt'))]
    psum x4 -> x0, blocking collectives: 73.4 us -> none  [the longest x1 38.1 us: shards(): lax.psum((local_img, local_txt, local_term), ('img', 'txt'))]
    reduce_scatter x2 -> x0, waiting for transfers between devices: 49 us -> none  [the longest x1 29.6 us: shards(): d_txt = lax.psum_scatter(part_txt, 'img', scatter_dimension=0, tiled=True)]
    all_gather x4 -> x0, blocking collectives: 46.9 us -> none  [the longest x1 14.5 us: shards(): lax.all_gather(text_feats, 'img', axis=0, tiled=True)]
    pallas_call x0 -> x2, Pallas kernels: none -> 38.2 us  [the longest x1 33.4 us: exchange(): pl.pallas_call(functools.partial(exchange_kernel, n_img, n_txt), out_shap...]
    pmax x2 -> x0, blocking collectives: 23.8 us -> none  [the longest x1 14.9 us: tile_terms(): ctm, csm = lax.pmax((tl.max(0), sl.max(0)), 'img')]
    dot_general x10 -> x0, matrix products: 9.06 us -> none  [the longest x2 5.23 us: weight_grad(): lax.dot_general(feats.astype(jnp.float32), du_rows, (((0,), (0,)), ((), (...]
    reduce_sum x8 -> x0, other arithmetic: 5.91 us -> none  [the longest x2 1.88 us: tangent(): jnp.sum(embeds * grad_rows, 1, keepdims=True)]
  transfers between devices with their start and end apart: 3 -> 0, of which waited for: 3 -> 0; matrix products, arithmetic and copies ran while one was open for 2% -> 0% of each run, Pallas kernels for 0% -> 0%
where the time goes in v2:
time: 39 us; the launch traced here: 38.8 us
  Pallas kernels  38.2 us (98%)
  between operations  0.64 us (2%)
    pallas_call x1, Pallas kernels, exchange(): pl.pallas_call(functools.partial(exchange_kernel, n_img, n_txt), out_shap...  33.4 us
    pallas_call x1, Pallas kernels, whole_batch(): pl.pallas_call(grads_kernel, out_shape=[jax.ShapeDtypeStruct((1, 1), f32)...  4.77 us

profile of v2, /device:TPU:0, one launch (start us, length us, event | category | flops | bytes accessed | tf_op | source)
XLA Modules:
  0.0 38.8 jit_solution(4402530852593382891)
XLA Ops:
  0.6 33.4 %exchange_and_embed.1 = (f32[1,1]{1,0:T(1,128)}, bf16[32,2,16,640]{3,2,1,0:T(8,128)(2,1)}, bf16[512,512]{1,0:T(8,128)(2,1)}, bf16[512,512]{1,0:T(8,128)(2,1)}) custom-call(bf16[16,768]{1,0:T(8,128)(2,1)} %image.1, bf16[16,512]{1,0:T(8,128)(2,1)} %text.1, bf16[16,1024]{1,0:T(8,128)(2,1)} %t_img.1, bf16[16,1024]{1,0:T(8,128)(2,1)} %t_txt.1, ...), custom_call_target="tpu_custom_call" | custom-call | tf_op jit(solution)/shard_map/exchange_and_embed/pallas_call | solution.py:447
  34.1 4.8 %weight_grads.1 = (f32[1,1]{1,0:T(1,128)}, f32[768,512]{1,0:T(8,128)}, f32[512,512]{1,0:T(8,128)}) custom-call(f32[1,1]{1,0:T(1,128)} %get-tuple-element.10.loss_in, bf16[32,2,16,640]{3,2,1,0:T(8,128)(2,1)} %get-tuple-element.11.feats_in, bf16[512,512]{1,0:T(8,128)(2,1)} %get-tuple-element.12.du_img_in, bf16[512,512]{1,0:T(8,128)(2,1)} %get-tuple-element.13.du_txt_in), custom_call_target="tpu_custom_call" | custom-call | tf_op jit(solution)/shard_map/weight_grads/pallas_call | solution.py:494

commit v3 on v2

--- a/solution.py
+++ b/solution.py
@@ -105,8 +105,8 @@
 
 
 class Spread:
-    def __init__(self, place, buf, halves, sems, log):
-        self.place, self.buf, self.halves, self.log = place, buf, halves, log
+    def __init__(self, place, buf, halves, sems, log, straight=False):
+        self.place, self.buf, self.halves, self.log, self.straight = place, buf, halves, log, straight
         self.sz, self.rz, self.sx, self.rx, self.sy, self.ry, self.sc, self.rc, self.sd, self.rd, self.se, self.re = sems
 
     def ref(self, at, part):
@@ -129,11 +129,10 @@
     def arrived(self, at, part, ssem, rsem):
         self.copy(at, part, self.place.partner, ssem, rsem).wait_recv()
 
-    def own(self):
+    def own_z(self):
         p = self.place
         for k in range(1, p.nz):
             self.send(p.slot(p.img, p.txt), None, p.z_peer(k), self.sz.at[k - 1], self.rz.at[k - 1])
-        self.line(0)
 
     def line(self, k):
         p = self.place
@@ -142,25 +141,32 @@
             self.arrived(at, None, self.sz.at[k - 1], self.rz.at[k - 1])
         self.send(at, None, (p.img, p.x_txt), self.sx.at[k], self.rx.at[k])
         self.send(at, None, (p.img, p.y_txt), self.sy.at[k], self.ry.at[k])
+        if self.straight:
+            self.send(at, None, (p.img, p.d_txt), self.sd.at[0, k], self.rd.at[0, k])
         self.send(at, None, p.partner, self.sc.at[0, k], self.rc.at[0, k])
 
     def turn(self, k):
         p = self.place
         at = p.slot(p.source(k), p.x_txt)
         self.arrived(at, None, self.sx.at[k], self.rx.at[k])
-        self.send(at, 0, (p.img, p.y_txt), self.sd.at[0, k], self.rd.at[0, k])
+        if not self.straight:
+            self.send(at, 0, (p.img, p.y_txt), self.sd.at[0, k], self.rd.at[0, k])
         self.send(at, None, p.partner, self.sc.at[1, k], self.rc.at[1, k])
         at = p.slot(p.source(k), p.y_txt)
         self.arrived(at, None, self.sy.at[k], self.ry.at[k])
-        self.send(at, 1, (p.img, p.x_txt), self.sd.at[1, k], self.rd.at[1, k])
+        if not self.straight:
+            self.send(at, 1, (p.img, p.x_txt), self.sd.at[1, k], self.rd.at[1, k])
         self.send(at, None, p.partner, self.sc.at[2, k], self.rc.at[2, k])
 
     def last(self, k):
         p = self.place
         at = p.slot(p.source(k), p.d_txt)
-        for part in range(2):
-            self.arrived(at, part, self.sd.at[part, k], self.rd.at[part, k])
-            self.send(at, part, p.partner, self.se.at[part, k], self.re.at[part, k])
+        for i, part in self.parts():
+            self.arrived(at, part, self.sd.at[i, k], self.rd.at[i, k])
+            self.send(at, part, p.partner, self.se.at[i, k], self.re.at[i, k])
+
+    def parts(self):
+        return ((0, None),) if self.straight else ((0, 0), (1, 1))
 
     def whole(self, which):
         p = self.place
@@ -170,8 +176,8 @@
                 at = p.slot(source, (p.txt, p.x_txt, p.y_txt)[which])
                 self.arrived(at, None, self.sc.at[which, k], self.rc.at[which, k])
             else:
-                for part in range(2):
-                    self.arrived(p.slot(source, p.d_txt), part, self.se.at[part, k], self.re.at[part, k])
+                for i, part in self.parts():
+                    self.arrived(p.slot(source, p.d_txt), part, self.se.at[i, k], self.re.at[i, k])
 
 
 class Place:
@@ -204,8 +210,9 @@
 
 
 def exchange_kernel(n_img, n_txt, image, text, t_img, t_txt, p_img, p_txt, *refs):
-    loss, feats_out, du_img_out, du_txt_out = refs[:4]
+    loss, turned_out, du_img_out, du_txt_out = refs[:4]
     feats, tiles, e_img, e_txt, i_img, i_txt, s_img, s_txt, sl, ps, du_img, du_txt = refs[4:16]
+    turned = refs[60]
     raw, q_img, q_txt, tile, row_st, col_st, w_img, w_txt, g_tile, load = refs[16:26]
     tz_s, tz_r, tc_s, tc_r, ti_s, ti_r, rs_s, rs_r, cs_s, cs_r = refs[26:36]
     f_sems, p_sems = refs[36:48], refs[48:60]
@@ -257,14 +264,18 @@
 
     f = Spread(p, feats, ((0, 1), (1, 2)), f_sems, log)
     rows_in, cols_in = rows * n_txt, rows * n_img
-    g = Spread(p, tiles, ((0, rows_in // 2), (rows_in // 2, rows_in + 16)), p_sems, log)
+    g = Spread(p, tiles, ((0, rows_in // 2), (rows_in // 2, rows_in + 16)), p_sems, log, straight=True)
 
     for k in range(1, nz):
         send(q_txt.at[img], p.z_peer(k), tz_s.at[k - 1], tz_r.at[k - 1])
     for k in range(1, n_txt):
         send(q_img.at[txt], (img, p.txt_at(k)), ti_s.at[k - 1], ti_r.at[k - 1])
     send(q_txt.at[img], p.partner, tc_s.at[0], tc_r.at[0])
-    f.own()
+    f.line(0)
+    for copy in log[: nz - 1]:
+        copy.wait_send()
+    del log[: nz - 1]
+    f.own_z()
     for k in range(1, nz):
         arrived(q_txt.at[p.source(k)], tz_s.at[k - 1], tz_r.at[k - 1])
         send(q_txt.at[p.source(k)], p.partner, tc_s.at[k], tc_r.at[k])
@@ -314,13 +325,16 @@
     pieces = jnp.where(line == 0, high, jnp.where(line == 1, middle, jnp.where(line == 2, part - high - middle, 0.0)))
     tiles[mine, 0:rows_in, :] = both.astype(jnp.bfloat16)
     tiles[mine, rows_in : rows_in + 16, :] = pieces.astype(jnp.bfloat16)
-    g.own()
+    g.own_z()
+    g.line(0)
 
     def embed(j):
         at = pl.ds(pl.multiple_of(j * cols_in, cols_in), cols_in)
         here = pl.ds(j * n_img, n_img)
         rest = feats[here, 1].reshape(cols_in, half)
         x = jnp.concatenate([feats[here, 0].reshape(cols_in, half), rest[:, 0 : fi - half]], axis=1)
+        turned[0:fi, at] = x.T
+        turned[fi : fi + ft, at] = rest[:, fi - half : half].T
         e, inv = project(x, w_img[...])
         e_img[at, :], i_img[at, :] = e, inv
         s_img[at, :] = e.astype(jnp.bfloat16)
@@ -346,14 +360,15 @@
     embed(p.y_txt)
     f.whole(3)
     embed(p.d_txt)
-    outs = [pltpu.make_async_copy(feats, feats_out, load.at[0])]
+    outs = [pltpu.make_async_copy(turned, turned_out, load.at[0])]
     outs[0].start()
     for k in range(nz):
         g.last(k)
 
-    def logits(c, carry):
-        csm, total = carry
-        at = pl.ds(pl.multiple_of(c * cols_in, cols_in), cols_in)
+    chunks = [slice(c * cols_in, (c + 1) * cols_in) for c in range(n_txt)]
+    csm = jnp.full((1, batch), -jnp.inf, jnp.float32)
+    total = jnp.zeros((1, 1), jnp.float32)
+    for at in chunks:
         s = STUDENT_SCALE * dot_nt(s_img[at, :], s_txt[...])
         sl[at, :] = s
         m = jnp.max(s, axis=1, keepdims=True)
@@ -361,46 +376,42 @@
         sums = jnp.sum(es, axis=1, keepdims=True)
         ps[at, :] = es * (1.0 / sums)
         total = total + jnp.sum(m + jnp.log(sums), axis=0, keepdims=True)
-        return jnp.maximum(csm, jnp.max(s, axis=0, keepdims=True)), total
-
-    low = jnp.full((1, batch), -jnp.inf, jnp.float32)
-    csm, total = lax.fori_loop(0, n_txt, logits, (low, jnp.zeros((1, 1), jnp.float32)))
-
-    def sums(c, css):
-        at = pl.ds(pl.multiple_of(c * cols_in, cols_in), cols_in)
-        return css + jnp.sum(jnp.exp(sl[at, :] - csm), axis=0, keepdims=True)
-
-    css = lax.fori_loop(0, n_txt, sums, jnp.zeros((1, batch), jnp.float32))
+        csm = jnp.maximum(csm, jnp.max(s, axis=0, keepdims=True))
+    css = jnp.zeros((1, batch), jnp.float32)
+    for at in chunks:
+        css = css + jnp.sum(jnp.exp(sl[at, :] - csm), axis=0, keepdims=True)
     lzc = csm + jnp.log(css)
     total = total + jnp.sum(lzc, axis=1, keepdims=True)
+    for at in chunks:
+        ps[at, :] = ps[at, :] + jnp.exp(sl[at, :] - lzc)
+    for copy in log:
+        copy.wait_send()
     for which in range(4):
         g.whole(which)
 
     def tile_rows(c):
-        held = [tiles[i * n_img : (i + 1) * n_img, pl.ds(pl.multiple_of(c * rows, rows), rows), :] for i in range(n_txt)]
+        held = [tiles[i * n_img : (i + 1) * n_img, c * rows : (c + 1) * rows, :] for i in range(n_txt)]
         return jnp.concatenate([h.reshape(cols_in, cols_in) for h in held], axis=1).astype(jnp.float32)
 
-    def gradient(c, terms):
-        at = pl.ds(pl.multiple_of(c * cols_in, cols_in), cols_in)
-        pt, s = tile_rows(c), sl[at, :]
-        g_tile[at, :] = (0.5 * STUDENT_SCALE * (ps[at, :] + jnp.exp(s - lzc) - pt)).astype(jnp.bfloat16)
-        return terms - jnp.sum(pt * s, axis=0, keepdims=True)
-
-    terms = lax.fori_loop(0, n_txt, gradient, jnp.zeros((1, batch), jnp.float32))
-    d_img = jnp.dot(g_tile[...], s_txt[...], preferred_element_type=jnp.float32)
-    du_img[...] = tangent(d_img, e_img[...], i_img[...]).astype(jnp.bfloat16)
+    terms = jnp.zeros((1, batch), jnp.float32)
+    for c, at in enumerate(chunks):
+        pt = tile_rows(c)
+        tile_g = (0.5 * STUDENT_SCALE * (ps[at, :] - pt)).astype(jnp.bfloat16)
+        g_tile[at, :] = tile_g
+        terms = terms - jnp.sum(pt * sl[at, :], axis=0, keepdims=True)
+        d_img = jnp.dot(tile_g, s_txt[...], preferred_element_type=jnp.float32)
+        du_img[at, :] = tangent(d_img, e_img[at, :], i_img[at, :]).astype(jnp.bfloat16)
     outs.append(pltpu.make_async_copy(du_img, du_img_out, load.at[1]))
     outs[1].start()
-    d_txt = dot_tn(g_tile[...], s_img[...])
-    du_txt[...] = tangent(d_txt, e_txt[...], i_txt[...]).astype(jnp.bfloat16)
+    for at in chunks:
+        d_txt = dot_tn(g_tile[:, at], s_img[...])
+        du_txt[at, :] = tangent(d_txt, e_txt[at, :], i_txt[at, :]).astype(jnp.bfloat16)
     outs.append(pltpu.make_async_copy(du_txt, du_txt_out, load.at[2]))
     outs[2].start()
     parts = jnp.sum(tiles[:, rows_in : rows_in + 16, :].astype(jnp.float32), axis=0)
     total = total + jnp.sum(terms, axis=1, keepdims=True)
     total = total + jnp.sum(jnp.sum(parts, axis=0, keepdims=True), axis=1, keepdims=True)
     loss[...] = total / (2.0 * batch)
-    for copy in log:
-        copy.wait_send()
     for copy in outs:
         copy.wait()
 
@@ -414,7 +425,7 @@
     dma = pltpu.SemaphoreType.DMA
     vmem = pl.BlockSpec(memory_space=pltpu.VMEM)
     hbm = pl.BlockSpec(memory_space=pltpu.HBM)
-    outs = [((1, 1), f32), ((slots, 2, rows, (fi + ft) // 2), b16), ((batch, ds), b16), ((batch, ds), b16)]
+    outs = [((1, 1), f32), ((fi + ft, batch), b16), ((batch, ds), b16), ((batch, ds), b16)]
     held = [
         ((slots, 2, rows, (fi + ft) // 2), b16),
         ((slots, rows_in + 16, cols_in), b16),
@@ -444,6 +455,7 @@
     spread = [(nz - 1,), (nz,), (nz,), (3, nz), (2, nz), (2, nz)]
     for shape in [(nz - 1,), (nz,), (n_txt - 1,), (n_txt - 1,), (n_img - 1,)] + spread + spread:
         scratch += [dma(shape), dma(shape)]
+    scratch.append(pltpu.VMEM((fi + ft, batch), b16))
     return pl.pallas_call(
         functools.partial(exchange_kernel, n_img, n_txt),
         out_shape=[jax.ShapeDtypeStruct(*s) for s in outs],
@@ -457,31 +469,40 @@
     )(image, text, t_img, t_txt, w_img, w_txt)
 
 
-def grads_kernel(loss_in, feats_in, du_img_in, du_txt_in, loss, grad_img, grad_txt, feats, du_img, du_txt, g_img, g_txt, load, store):
-    slots, _, rows, half = feats.shape
-    batch = slots * rows
-    fi = grad_img.shape[0]
+def grads_kernel(loss_in, turned_in, du_img_in, du_txt_in, loss, grad_img, grad_txt, turned, du_img, du_txt, g_img, g_txt, load, store):
+    fi, ft = grad_img.shape[0], grad_txt.shape[0]
+    step = LANES * 2
     loads = [
         pltpu.make_async_copy(du_img_in, du_img, load.at[0]),
-        pltpu.make_async_copy(feats_in, feats, load.at[1]),
-        pltpu.make_async_copy(du_txt_in, du_txt, load.at[2]),
+        pltpu.make_async_copy(turned_in.at[0:step], turned.at[0:step], load.at[1]),
+        pltpu.make_async_copy(turned_in.at[step : fi + ft], turned.at[step : fi + ft], load.at[2]),
+        pltpu.make_async_copy(du_txt_in, du_txt, load.at[3]),
     ]
     for copy in loads:
         copy.start()
     loss[...] = loss_in[...]
+    stores = []
+
+    def block(lo, at, du, held, out):
+        rows = min(step, held.shape[0] - at)
+        here = slice(at, at + rows)
+        held[here, :] = jnp.dot(turned[lo + at : lo + at + rows, :], du[...], preferred_element_type=jnp.float32)
+        copy = pltpu.make_async_copy(held.at[here], out.at[here], store.at[len(stores)])
+        copy.start()
+        stores.append(copy)
+
     for copy in loads[:2]:
         copy.wait()
-    g_img[0:half, :] = dot_tn(feats[:, 0].reshape(batch, half), du_img[...])
-    first = pltpu.make_async_copy(g_img.at[0:half], grad_img.at[0:half], store.at[0])
-    first.start()
-    g_img[half:fi, :] = dot_tn(feats[:, 1, :, 0 : fi - half].reshape(batch, fi - half), du_img[...])
-    second = pltpu.make_async_copy(g_img.at[half:fi], grad_img.at[half:fi], store.at[1])
-    second.start()
-    loads[2].wait()
-    g_txt[...] = dot_tn(feats[:, 1, :, fi - half : half].reshape(batch, 2 * half - fi), du_txt[...])
-    third = pltpu.make_async_copy(g_txt, grad_txt, store.at[2])
-    third.start()
-    for copy in (first, second, third):
+    for at in range(0, fi, step):
+        if at == step:
+            loads[2].wait()
+        block(0, at, du_img, g_img, grad_img)
+    if fi <= step:
+        loads[2].wait()
+    loads[3].wait()
+    for at in range(0, ft, step):
+        block(fi, at, du_txt, g_txt, grad_txt)
+    for copy in stores:
         copy.wait()
 
 
@@ -504,8 +525,8 @@
         + [
             pltpu.VMEM((fi, ds), f32),
             pltpu.VMEM((ft, ds), f32),
-            pltpu.SemaphoreType.DMA((3,)),
-            pltpu.SemaphoreType.DMA((3,)),
+            pltpu.SemaphoreType.DMA((4,)),
+            pltpu.SemaphoreType.DMA((pl.cdiv(fi, LANES * 2) + pl.cdiv(ft, LANES * 2),)),
         ],
         compiler_params=pltpu.CompilerParams(vmem_limit_bytes=FUSED_VMEM_BYTES),
         name="weight_grads",

time: 39 us -> 35.2 us (0.903)
  Pallas kernels: 38.2 us -> 34.4 us
    pallas_call x1, Pallas kernels: 33.4 us -> 30 us  [exchange(): pl.pallas_call(functools.partial(exchange_kernel, n_img, n_txt), out_shap...]
where the time goes in v3:
time: 35.2 us; the launch traced here: 35 us
  Pallas kernels  34.4 us (98%)
  between operations  0.64 us (2%)
    pallas_call x1, Pallas kernels, exchange(): pl.pallas_call(functools.partial(exchange_kernel, n_img, n_txt), out_shap...  30 us
    pallas_call x1, Pallas kernels, whole_batch(): pl.pallas_call(grads_kernel, out_shape=[jax.ShapeDtypeStruct((1, 1), f32)...  4.45 us

profile of v3, /device:TPU:0, one launch (start us, length us, event | category | flops | bytes accessed | tf_op | source)
XLA Modules:
  0.0 35.0 jit_solution(13216951883373700189)
XLA Ops:
  0.6 30.0 %exchange_and_embed.1 = (f32[1,1]{1,0:T(1,128)}, bf16[1280,512]{1,0:T(8,128)(2,1)}, bf16[512,512]{1,0:T(8,128)(2,1)}, bf16[512,512]{1,0:T(8,128)(2,1)}) custom-call(bf16[16,768]{1,0:T(8,128)(2,1)} %image.1, bf16[16,512]{1,0:T(8,128)(2,1)} %text.1, bf16[16,1024]{1,0:T(8,128)(2,1)} %t_img.1, bf16[16,1024]{1,0:T(8,128)(2,1)} %t_txt.1, bf16[768,512]{1,0:T(8,128)(2,1)} %p_img.1, ...), custom_call_target="tpu_custom_call" | custom-call | tf_op jit(solution)/shard_map/exchange_and_embed/pallas_call | solution.py:459
  30.6 4.4 %weight_grads.1 = (f32[1,1]{1,0:T(1,128)}, f32[768,512]{1,0:T(8,128)}, f32[512,512]{1,0:T(8,128)}) custom-call(f32[1,1]{1,0:T(1,128)} %get-tuple-element.10.loss_in, bf16[1280,512]{1,0:T(8,128)(2,1)} %get-tuple-element.11.turned_in, bf16[512,512]{1,0:T(8,128)(2,1)} %get-tuple-element.12.du_img_in, bf16[512,512]{1,0:T(8,128)(2,1)} %get-tuple-element.13.du_txt_in), custom_call_target="tpu_custom_call" | custom-call | tf_op jit(solution)/shard_map/weight_grads/pallas_call | solution.py:515

commit v4 on v3

--- a/solution.py
+++ b/solution.py
@@ -104,15 +104,31 @@
     return lax.dot_general(a, b, (((0,), (0,)), ((), ())), preferred_element_type=jnp.float32)
 
 
+def bf16_pieces(x):
+    high = x.astype(jnp.bfloat16).astype(jnp.float32)
+    middle = (x - high).astype(jnp.bfloat16).astype(jnp.float32)
+    return [high, middle, x - high - middle]
+
+
+def at_places(index, values):
+    out = jnp.zeros(index.shape, jnp.float32)
+    for i, value in enumerate(values):
+        out = jnp.where(index == i, value, out)
+    return out.astype(jnp.bfloat16)
+
+
 class Spread:
-    def __init__(self, place, buf, halves, sems, log, straight=False):
-        self.place, self.buf, self.halves, self.log, self.straight = place, buf, halves, log, straight
+    def __init__(self, place, buf, halves, sems, log, straight=False, columns=False):
+        self.place, self.buf, self.halves, self.log = place, buf, halves, log
+        self.straight, self.columns = straight, columns
         self.sz, self.rz, self.sx, self.rx, self.sy, self.ry, self.sc, self.rc, self.sd, self.rd, self.se, self.re = sems
 
     def ref(self, at, part):
         if part is None:
             return self.buf.at[at]
         lo, hi = self.halves[part]
+        if self.columns:
+            return self.buf.at[at, :, lo:hi]
         return self.buf.at[at, lo:hi]
 
     def copy(self, at, part, peer, ssem, rsem):
@@ -210,16 +226,15 @@
 
 
 def exchange_kernel(n_img, n_txt, image, text, t_img, t_txt, p_img, p_txt, *refs):
-    loss, turned_out, du_img_out, du_txt_out = refs[:4]
-    feats, tiles, e_img, e_txt, i_img, i_txt, s_img, s_txt, sl, ps, du_img, du_txt = refs[4:16]
-    turned = refs[60]
-    raw, q_img, q_txt, tile, row_st, col_st, w_img, w_txt, g_tile, load = refs[16:26]
-    tz_s, tz_r, tc_s, tc_r, ti_s, ti_r, rs_s, rs_r, cs_s, cs_r = refs[26:36]
-    f_sems, p_sems = refs[36:48], refs[48:60]
+    loss, feats_out, du_img_out, du_txt_out = refs[:4]
+    feats, tiles, embeds, sl, ps, du_img, du_txt = refs[4:11]
+    raw, q_img, q_txt, tile, row_st, col_st, w_img, w_txt, g_tile, load = refs[11:21]
+    tz_s, tz_r, tc_s, tc_r, ti_s, ti_r, rs_s, rs_r, cs_s, cs_r = refs[21:31]
+    f_sems, p_sems, e_sems = refs[31:43], refs[43:55], refs[55:67]
     p = Place(n_img, n_txt)
     nz, img, txt = p.nz, p.img, p.txt
     rows, fi = image.shape
-    ft, dt = text.shape[1], t_img.shape[1]
+    ft, dt, ds = text.shape[1], t_img.shape[1], p_img.shape[1]
     half = feats.shape[3]
     batch = sl.shape[0]
     mine = p.slot(img, txt)
@@ -243,8 +258,16 @@
     q_img[txt] = normed(raw[0])
     loads[1].wait()
     q_txt[img] = normed(raw[1])
-    for copy in loads[2:5]:
+    for copy in loads[2:]:
         copy.wait()
+    own = feats[mine, 1]
+    e, inv = project(jnp.concatenate([feats[mine, 0], own[:, 0 : fi - half]], axis=1), w_img[...])
+    embeds[mine, :, 0:ds] = e.astype(jnp.bfloat16)
+    pieces = bf16_pieces(inv)
+    e, inv = project(own[:, fi - half : half], w_txt[...])
+    embeds[mine, :, ds + LANES :] = e.astype(jnp.bfloat16)
+    lane = lax.broadcasted_iota(jnp.int32, (rows, LANES), 1)
+    embeds[mine, :, ds : ds + LANES] = at_places(lane, pieces + bf16_pieces(inv))
     pl.semaphore_wait(barrier, len(peers))
 
     log = []
@@ -263,6 +286,7 @@
         copy_of(ref, p.partner, ssem, rsem).wait_recv()
 
     f = Spread(p, feats, ((0, 1), (1, 2)), f_sems, log)
+    e = Spread(p, embeds, ((0, ds + LANES), (ds + LANES, 2 * ds + LANES)), e_sems, log, columns=True)
     rows_in, cols_in = rows * n_txt, rows * n_img
     g = Spread(p, tiles, ((0, rows_in // 2), (rows_in // 2, rows_in + 16)), p_sems, log, straight=True)
 
@@ -271,11 +295,11 @@
     for k in range(1, n_txt):
         send(q_img.at[txt], (img, p.txt_at(k)), ti_s.at[k - 1], ti_r.at[k - 1])
     send(q_txt.at[img], p.partner, tc_s.at[0], tc_r.at[0])
-    f.line(0)
+    e.line(0)
     for copy in log[: nz - 1]:
         copy.wait_send()
     del log[: nz - 1]
-    f.own_z()
+    e.own_z()
     for k in range(1, nz):
         arrived(q_txt.at[p.source(k)], tz_s.at[k - 1], tz_r.at[k - 1])
         send(q_txt.at[p.source(k)], p.partner, tc_s.at[k], tc_r.at[k])
@@ -303,7 +327,8 @@
         send(row_st.at[txt], (img, p.txt_at(k)), rs_s.at[k - 1], rs_r.at[k - 1])
 
     for k in range(1, nz):
-        f.line(k)
+        e.line(k)
+    f.own_z()
     for k in range(1, n_img):
         arrived(col_st.at[p.img_at(n_img - k)], cs_s.at[k - 1], cs_r.at[k - 1])
     for k in range(1, n_txt):
@@ -319,57 +344,42 @@
     both = jnp.exp(t - jnp.broadcast_to(lz_row, (cols_in, rows_in)).T) + jnp.exp(t - lz_col)
     part = jnp.sum(both * t, axis=0, keepdims=True) - lz_col / n_img
     part = part - jnp.sum(lz_row, axis=1, keepdims=True) / (n_txt * cols_in)
-    high = part.astype(jnp.bfloat16).astype(jnp.float32)
-    middle = (part - high).astype(jnp.bfloat16).astype(jnp.float32)
     line = lax.broadcasted_iota(jnp.int32, (16, cols_in), 0)
-    pieces = jnp.where(line == 0, high, jnp.where(line == 1, middle, jnp.where(line == 2, part - high - middle, 0.0)))
     tiles[mine, 0:rows_in, :] = both.astype(jnp.bfloat16)
-    tiles[mine, rows_in : rows_in + 16, :] = pieces.astype(jnp.bfloat16)
+    tiles[mine, rows_in : rows_in + 16, :] = at_places(line, bf16_pieces(part))
     g.own_z()
     g.line(0)
 
-    def embed(j):
-        at = pl.ds(pl.multiple_of(j * cols_in, cols_in), cols_in)
-        here = pl.ds(j * n_img, n_img)
-        rest = feats[here, 1].reshape(cols_in, half)
-        x = jnp.concatenate([feats[here, 0].reshape(cols_in, half), rest[:, 0 : fi - half]], axis=1)
-        turned[0:fi, at] = x.T
-        turned[fi : fi + ft, at] = rest[:, fi - half : half].T
-        e, inv = project(x, w_img[...])
-        e_img[at, :], i_img[at, :] = e, inv
-        s_img[at, :] = e.astype(jnp.bfloat16)
-        e, inv = project(rest[:, fi - half : half], w_txt[...])
-        e_txt[at, :], i_txt[at, :] = e, inv
-        s_txt[at, :] = e.astype(jnp.bfloat16)
-
-    for k in range(nz):
-        f.turn(k)
-    f.whole(0)
-    for copy in loads[5:]:
-        copy.wait()
-    embed(txt)
+    for k in range(nz):
+        e.turn(k)
+    f.line(0)
     for k in range(1, nz):
         g.line(k)
     for k in range(nz):
-        f.last(k)
-    f.whole(1)
-    embed(p.x_txt)
-    for k in range(nz):
-        g.turn(k)
-    f.whole(2)
-    embed(p.y_txt)
-    f.whole(3)
-    embed(p.d_txt)
-    outs = [pltpu.make_async_copy(turned, turned_out, load.at[0])]
-    outs[0].start()
-    for k in range(nz):
-        g.last(k)
+        e.last(k)
+    for k in range(1, nz):
+        f.line(k)
+    for which in range(4):
+        e.whole(which)
+
+    def s_img(c):
+        return embeds[c * n_img : (c + 1) * n_img, :, 0:ds].reshape(cols_in, ds)
+
+    def s_txt(c):
+        return embeds[c * n_img : (c + 1) * n_img, :, ds + LANES :].reshape(cols_in, ds)
+
+    def inverse(c, at):
+        held = embeds[c * n_img : (c + 1) * n_img, :, ds : ds + LANES].reshape(cols_in, LANES).astype(jnp.float32)
+        return held[:, at : at + 1] + held[:, at + 1 : at + 2] + held[:, at + 2 : at + 3]
+
+    def all_txt():
+        return embeds[:, :, ds + LANES :].reshape(batch, ds)
 
     chunks = [slice(c * cols_in, (c + 1) * cols_in) for c in range(n_txt)]
     csm = jnp.full((1, batch), -jnp.inf, jnp.float32)
     total = jnp.zeros((1, 1), jnp.float32)
-    for at in chunks:
-        s = STUDENT_SCALE * dot_nt(s_img[at, :], s_txt[...])
+    for c, at in enumerate(chunks):
+        s = STUDENT_SCALE * dot_nt(s_img(c), all_txt())
         sl[at, :] = s
         m = jnp.max(s, axis=1, keepdims=True)
         es = jnp.exp(s - m)
@@ -384,8 +394,15 @@
     total = total + jnp.sum(lzc, axis=1, keepdims=True)
     for at in chunks:
         ps[at, :] = ps[at, :] + jnp.exp(sl[at, :] - lzc)
+    for k in range(nz):
+        g.turn(k)
+    for k in range(nz):
+        g.last(k)
+    for k in range(nz):
+        f.turn(k)
     for copy in log:
         copy.wait_send()
+    del log[:]
     for which in range(4):
         g.whole(which)
 
@@ -399,19 +416,27 @@
         tile_g = (0.5 * STUDENT_SCALE * (ps[at, :] - pt)).astype(jnp.bfloat16)
         g_tile[at, :] = tile_g
         terms = terms - jnp.sum(pt * sl[at, :], axis=0, keepdims=True)
-        d_img = jnp.dot(tile_g, s_txt[...], preferred_element_type=jnp.float32)
-        du_img[at, :] = tangent(d_img, e_img[at, :], i_img[at, :]).astype(jnp.bfloat16)
-    outs.append(pltpu.make_async_copy(du_img, du_img_out, load.at[1]))
+        d_img = jnp.dot(tile_g, all_txt(), preferred_element_type=jnp.float32)
+        du_img[at, :] = tangent(d_img, s_img(c).astype(jnp.float32), inverse(c, 0)).astype(jnp.bfloat16)
+    outs = [pltpu.make_async_copy(du_img, du_img_out, load.at[1])]
+    outs[0].start()
+    for k in range(nz):
+        f.last(k)
+    for c, at in enumerate(chunks):
+        d_txt = dot_tn(g_tile[:, at], embeds[:, :, 0:ds].reshape(batch, ds))
+        du_txt[at, :] = tangent(d_txt, s_txt(c).astype(jnp.float32), inverse(c, 3)).astype(jnp.bfloat16)
+    outs.append(pltpu.make_async_copy(du_txt, du_txt_out, load.at[2]))
     outs[1].start()
-    for at in chunks:
-        d_txt = dot_tn(g_tile[:, at], s_img[...])
-        du_txt[at, :] = tangent(d_txt, e_txt[at, :], i_txt[at, :]).astype(jnp.bfloat16)
-    outs.append(pltpu.make_async_copy(du_txt, du_txt_out, load.at[2]))
+    for which in range(4):
+        f.whole(which)
+    outs.append(pltpu.make_async_copy(feats, feats_out, load.at[0]))
     outs[2].start()
     parts = jnp.sum(tiles[:, rows_in : rows_in + 16, :].astype(jnp.float32), axis=0)
     total = total + jnp.sum(terms, axis=1, keepdims=True)
     total = total + jnp.sum(jnp.sum(parts, axis=0, keepdims=True), axis=1, keepdims=True)
     loss[...] = total / (2.0 * batch)
+    for copy in log:
+        copy.wait_send()
     for copy in outs:
         copy.wait()
 
@@ -425,16 +450,11 @@
     dma = pltpu.SemaphoreType.DMA
     vmem = pl.BlockSpec(memory_space=pltpu.VMEM)
     hbm = pl.BlockSpec(memory_space=pltpu.HBM)
-    outs = [((1, 1), f32), ((fi + ft, batch), b16), ((batch, ds), b16), ((batch, ds), b16)]
+    outs = [((1, 1), f32), ((slots, 2, rows, (fi + ft) // 2), b16), ((batch, ds), b16), ((batch, ds), b16)]
     held = [
         ((slots, 2, rows, (fi + ft) // 2), b16),
         ((slots, rows_in + 16, cols_in), b16),
-        ((batch, ds), f32),
-        ((batch, ds), f32),
-        ((batch, 1), f32),
-        ((batch, 1), f32),
-        ((batch, ds), b16),
-        ((batch, ds), b16),
+        ((slots, rows, 2 * ds + LANES), b16),
         ((batch, batch), f32),
         ((batch, batch), f32),
         ((batch, ds), b16),
@@ -453,9 +473,8 @@
         dma((7,)),
     ]
     spread = [(nz - 1,), (nz,), (nz,), (3, nz), (2, nz), (2, nz)]
-    for shape in [(nz - 1,), (nz,), (n_txt - 1,), (n_txt - 1,), (n_img - 1,)] + spread + spread:
+    for shape in [(nz - 1,), (nz,), (n_txt - 1,), (n_txt - 1,), (n_img - 1,)] + spread * 3:
         scratch += [dma(shape), dma(shape)]
-    scratch.append(pltpu.VMEM((fi + ft, batch), b16))
     return pl.pallas_call(
         functools.partial(exchange_kernel, n_img, n_txt),
         out_shape=[jax.ShapeDtypeStruct(*s) for s in outs],
@@ -465,17 +484,19 @@
         compiler_params=pltpu.CompilerParams(
             collective_id=0, has_side_effects=True, vmem_limit_bytes=FUSED_VMEM_BYTES
         ),
-        name="exchange_and_embed",
+        name="embed_and_exchange",
     )(image, text, t_img, t_txt, w_img, w_txt)
 
 
-def grads_kernel(loss_in, turned_in, du_img_in, du_txt_in, loss, grad_img, grad_txt, turned, du_img, du_txt, g_img, g_txt, load, store):
+def grads_kernel(loss_in, feats_in, du_img_in, du_txt_in, loss, grad_img, grad_txt, feats, du_img, du_txt, g_img, g_txt, load, store):
+    slots, _, rows, half = feats.shape
+    batch = slots * rows
     fi, ft = grad_img.shape[0], grad_txt.shape[0]
     step = LANES * 2
     loads = [
         pltpu.make_async_copy(du_img_in, du_img, load.at[0]),
-        pltpu.make_async_copy(turned_in.at[0:step], turned.at[0:step], load.at[1]),
-        pltpu.make_async_copy(turned_in.at[step : fi + ft], turned.at[step : fi + ft], load.at[2]),
+        pltpu.make_async_copy(feats_in.at[:, 0], feats.at[:, 0], load.at[1]),
+        pltpu.make_async_copy(feats_in.at[:, 1], feats.at[:, 1], load.at[2]),
         pltpu.make_async_copy(du_txt_in, du_txt, load.at[3]),
     ]
     for copy in loads:
@@ -483,25 +504,22 @@
     loss[...] = loss_in[...]
     stores = []
 
-    def block(lo, at, du, held, out):
-        rows = min(step, held.shape[0] - at)
-        here = slice(at, at + rows)
-        held[here, :] = jnp.dot(turned[lo + at : lo + at + rows, :], du[...], preferred_element_type=jnp.float32)
+    def block(part, lo, hi, at, du, held, out):
+        here = slice(at, at + hi - lo)
+        held[here, :] = dot_tn(feats[:, part, :, lo:hi].reshape(batch, hi - lo), du[...])
         copy = pltpu.make_async_copy(held.at[here], out.at[here], store.at[len(stores)])
         copy.start()
         stores.append(copy)
 
     for copy in loads[:2]:
         copy.wait()
-    for at in range(0, fi, step):
-        if at == step:
-            loads[2].wait()
-        block(0, at, du_img, g_img, grad_img)
-    if fi <= step:
-        loads[2].wait()
+    for lo in range(0, half, step):
+        block(0, lo, min(lo + step, half), lo, du_img, g_img, grad_img)
+    loads[2].wait()
+    block(1, 0, fi - half, half, du_img, g_img, grad_img)
     loads[3].wait()
-    for at in range(0, ft, step):
-        block(fi, at, du_txt, g_txt, grad_txt)
+    for lo in range(0, ft, step):
+        block(1, fi - half + lo, fi - half + min(lo + step, ft), lo, du_txt, g_txt, grad_txt)
     for copy in stores:
         copy.wait()
 
@@ -526,7 +544,7 @@
             pltpu.VMEM((fi, ds), f32),
             pltpu.VMEM((ft, ds), f32),
             pltpu.SemaphoreType.DMA((4,)),
-            pltpu.SemaphoreType.DMA((pl.cdiv(fi, LANES * 2) + pl.cdiv(ft, LANES * 2),)),
+            pltpu.SemaphoreType.DMA((pl.cdiv(held[1].shape[3], LANES * 2) + 1 + pl.cdiv(ft, LANES * 2),)),
         ],
         compiler_params=pltpu.CompilerParams(vmem_limit_bytes=FUSED_VMEM_BYTES),
         name="weight_grads",

time: 35.2 us -> 41 us (1.16)
  Pallas kernels: 34.4 us -> 40.1 us
    pallas_call x1, Pallas kernels: 30 us -> 35.5 us  [exchange(): pl.pallas_call(functools.partial(exchange_kernel, n_img, n_txt), out_shap...]
where the time goes in v4:
time: 41 us; the launch traced here: 40.8 us
  Pallas kernels  40.1 us (98%)
  between operations  0.64 us (2%)
    pallas_call x1, Pallas kernels, exchange(): pl.pallas_call(functools.partial(exchange_kernel, n_img, n_txt), out_shap...  35.5 us
    pallas_call x1, Pallas kernels, whole_batch(): pl.pallas_call(grads_kernel, out_shape=[jax.ShapeDtypeStruct((1, 1), f32)...  4.62 us

profile of v4, /device:TPU:0, one launch (start us, length us, event | category | flops | bytes accessed | tf_op | source)
XLA Modules:
  0.0 40.8 jit_solution(15965973660362484242)
XLA Ops:
  0.6 35.5 %embed_and_exchange.1 = (f32[1,1]{1,0:T(1,128)}, bf16[32,2,16,640]{3,2,1,0:T(8,128)(2,1)}, bf16[512,512]{1,0:T(8,128)(2,1)}, bf16[512,512]{1,0:T(8,128)(2,1)}) custom-call(bf16[16,768]{1,0:T(8,128)(2,1)} %image.1, bf16[16,512]{1,0:T(8,128)(2,1)} %text.1, bf16[16,1024]{1,0:T(8,128)(2,1)} %t_img.1, bf16[16,1024]{1,0:T(8,128)(2,1)} %t_txt.1, ...), custom_call_target="tpu_custom_call" | custom-call | tf_op jit(solution)/shard_map/embed_and_exchange/pallas_call | solution.py:478
  36.2 4.6 %weight_grads.1 = (f32[1,1]{1,0:T(1,128)}, f32[768,512]{1,0:T(8,128)}, f32[512,512]{1,0:T(8,128)}) custom-call(f32[1,1]{1,0:T(1,128)} %get-tuple-element.10.loss_in, bf16[32,2,16,640]{3,2,1,0:T(8,128)(2,1)} %get-tuple-element.11.feats_in, bf16[512,512]{1,0:T(8,128)(2,1)} %get-tuple-element.12.du_img_in, bf16[512,512]{1,0:T(8,128)(2,1)} %get-tuple-element.13.du_txt_in), custom_call_target="tpu_custom_call" | custom-call | tf_op jit(solution)/shard_map/weight_grads/pallas_call | solution.py:533

commit v5 on v3

--- a/solution.py
+++ b/solution.py
@@ -107,16 +107,14 @@
 class Spread:
     def __init__(self, place, buf, halves, sems, log, straight=False):
         self.place, self.buf, self.halves, self.log, self.straight = place, buf, halves, log, straight
-        self.sz, self.rz, self.sx, self.rx, self.sy, self.ry, self.sc, self.rc, self.sd, self.rd, self.se, self.re = sems
-
-    def ref(self, at, part):
+        self.sz, self.rz, self.sl, self.rl, self.sc, self.rc = sems
+
+    def copy(self, at, part, peer, ssem, rsem):
         if part is None:
-            return self.buf.at[at]
-        lo, hi = self.halves[part]
-        return self.buf.at[at, lo:hi]
-
-    def copy(self, at, part, peer, ssem, rsem):
-        ref = self.ref(at, part)
+            ref = self.buf.at[at]
+        else:
+            lo, hi = self.halves[part]
+            ref = self.buf.at[at, lo:hi]
         return pltpu.make_async_remote_copy(
             src_ref=ref, dst_ref=ref, send_sem=ssem, recv_sem=rsem, device_id=peer, device_id_type=MESH
         )
@@ -134,50 +132,40 @@
         for k in range(1, p.nz):
             self.send(p.slot(p.img, p.txt), None, p.z_peer(k), self.sz.at[k - 1], self.rz.at[k - 1])
 
-    def line(self, k):
+    def line(self):
         p = self.place
-        at = p.slot(p.source(k), p.txt)
-        if k > 0:
-            self.arrived(at, None, self.sz.at[k - 1], self.rz.at[k - 1])
-        self.send(at, None, (p.img, p.x_txt), self.sx.at[k], self.rx.at[k])
-        self.send(at, None, (p.img, p.y_txt), self.sy.at[k], self.ry.at[k])
+        for k in range(1, p.nz):
+            self.arrived(p.slot(p.source(k), p.txt), None, self.sz.at[k - 1], self.rz.at[k - 1])
+        at = p.line(p.img, p.txt)
         if self.straight:
-            self.send(at, None, (p.img, p.d_txt), self.sd.at[0, k], self.rd.at[0, k])
-        self.send(at, None, p.partner, self.sc.at[0, k], self.rc.at[0, k])
-
-    def turn(self, k):
+            self.send(at, None, (p.img, p.d_txt), self.sl.at[2], self.rl.at[2])
+        self.send(at, None, (p.img, p.x_txt), self.sl.at[0], self.rl.at[0])
+        self.send(at, None, (p.img, p.y_txt), self.sl.at[1], self.rl.at[1])
+        self.send(at, None, p.partner, self.sc.at[0], self.rc.at[0])
+
+    def turn(self):
         p = self.place
-        at = p.slot(p.source(k), p.x_txt)
-        self.arrived(at, None, self.sx.at[k], self.rx.at[k])
-        if not self.straight:
-            self.send(at, 0, (p.img, p.y_txt), self.sd.at[0, k], self.rd.at[0, k])
-        self.send(at, None, p.partner, self.sc.at[1, k], self.rc.at[1, k])
-        at = p.slot(p.source(k), p.y_txt)
-        self.arrived(at, None, self.sy.at[k], self.ry.at[k])
-        if not self.straight:
-            self.send(at, 1, (p.img, p.x_txt), self.sd.at[1, k], self.rd.at[1, k])
-        self.send(at, None, p.partner, self.sc.at[2, k], self.rc.at[2, k])
-
-    def last(self, k):
+        for i, (near, far) in enumerate([(p.x_txt, p.y_txt), (p.y_txt, p.x_txt)]):
+            at = p.line(p.img, near)
+            self.arrived(at, None, self.sl.at[i], self.rl.at[i])
+            if not self.straight:
+                self.send(at, i, (p.img, far), self.sl.at[2 + i], self.rl.at[2 + i])
+            self.send(at, None, p.partner, self.sc.at[1 + i], self.rc.at[1 + i])
+
+    def last(self):
         p = self.place
-        at = p.slot(p.source(k), p.d_txt)
+        at = p.line(p.img, p.d_txt)
         for i, part in self.parts():
-            self.arrived(at, part, self.sd.at[i, k], self.rd.at[i, k])
-            self.send(at, part, p.partner, self.se.at[i, k], self.re.at[i, k])
+            self.arrived(at, part, self.sl.at[2 + i], self.rl.at[2 + i])
+        self.send(at, None, p.partner, self.sc.at[3], self.rc.at[3])
 
     def parts(self):
         return ((0, None),) if self.straight else ((0, 0), (1, 1))
 
     def whole(self, which):
         p = self.place
-        for k in range(p.nz):
-            source = p.other_source(k)
-            if which < 3:
-                at = p.slot(source, (p.txt, p.x_txt, p.y_txt)[which])
-                self.arrived(at, None, self.sc.at[which, k], self.rc.at[which, k])
-            else:
-                for i, part in self.parts():
-                    self.arrived(p.slot(source, p.d_txt), part, self.se.at[i, k], self.re.at[i, k])
+        at = p.line(p.other, (p.txt, p.x_txt, p.y_txt, p.d_txt)[which])
+        self.arrived(at, None, self.sc.at[which], self.rc.at[which])
 
 
 class Place:
@@ -190,8 +178,14 @@
         self.y_txt = lax.rem(self.txt + 2, 4)
         self.d_txt = lax.rem(self.x_txt + 2, 4)
 
+    def order(self, img):
+        return lax.rem(img, 2) * self.nz + img // 2
+
     def slot(self, img, txt):
-        return txt * self.n_img + img
+        return txt * self.n_img + self.order(img)
+
+    def line(self, img, txt):
+        return pl.ds(txt * self.n_img + lax.rem(img, 2) * self.nz, self.nz)
 
     def source(self, k):
         return lax.rem(self.img + self.n_img - 2 * k, self.n_img)
@@ -210,12 +204,12 @@
 
 
 def exchange_kernel(n_img, n_txt, image, text, t_img, t_txt, p_img, p_txt, *refs):
-    loss, turned_out, du_img_out, du_txt_out = refs[:4]
+    loss_out, turned_out, du_img_out, du_txt_out = refs[:4]
     feats, tiles, e_img, e_txt, i_img, i_txt, s_img, s_txt, sl, ps, du_img, du_txt = refs[4:16]
-    turned = refs[60]
+    turned, loss = refs[48:50]
     raw, q_img, q_txt, tile, row_st, col_st, w_img, w_txt, g_tile, load = refs[16:26]
     tz_s, tz_r, tc_s, tc_r, ti_s, ti_r, rs_s, rs_r, cs_s, cs_r = refs[26:36]
-    f_sems, p_sems = refs[36:48], refs[48:60]
+    f_sems, p_sems = refs[36:42], refs[42:48]
     p = Place(n_img, n_txt)
     nz, img, txt = p.nz, p.img, p.txt
     rows, fi = image.shape
@@ -242,7 +236,8 @@
     loads[0].wait()
     q_img[txt] = normed(raw[0])
     loads[1].wait()
-    q_txt[img] = normed(raw[1])
+    mine_q = p.order(img)
+    q_txt[mine_q] = normed(raw[1])
     for copy in loads[2:5]:
         copy.wait()
     pl.semaphore_wait(barrier, len(peers))
@@ -267,22 +262,19 @@
     g = Spread(p, tiles, ((0, rows_in // 2), (rows_in // 2, rows_in + 16)), p_sems, log, straight=True)
 
     for k in range(1, nz):
-        send(q_txt.at[img], p.z_peer(k), tz_s.at[k - 1], tz_r.at[k - 1])
+        send(q_txt.at[mine_q], p.z_peer(k), tz_s.at[k - 1], tz_r.at[k - 1])
     for k in range(1, n_txt):
         send(q_img.at[txt], (img, p.txt_at(k)), ti_s.at[k - 1], ti_r.at[k - 1])
-    send(q_txt.at[img], p.partner, tc_s.at[0], tc_r.at[0])
-    f.line(0)
     for copy in log[: nz - 1]:
         copy.wait_send()
     del log[: nz - 1]
     f.own_z()
     for k in range(1, nz):
-        arrived(q_txt.at[p.source(k)], tz_s.at[k - 1], tz_r.at[k - 1])
-        send(q_txt.at[p.source(k)], p.partner, tc_s.at[k], tc_r.at[k])
+        arrived(q_txt.at[p.order(p.source(k))], tz_s.at[k - 1], tz_r.at[k - 1])
+    send(q_txt.at[p.line(img, 0)], p.partner, tc_s.at[0], tc_r.at[0])
     for k in range(1, n_txt):
         arrived(q_img.at[p.txt_at(n_txt - k)], ti_s.at[k - 1], ti_r.at[k - 1])
-    for k in range(nz):
-        arrived(q_txt.at[p.other_source(k)], tc_s.at[k], tc_r.at[k])
+    arrived(q_txt.at[p.line(p.other, 0)], tc_s.at[0], tc_r.at[0])
 
     t = TEACHER_SCALE * dot_nt(q_img[...].reshape(rows_in, dt), q_txt[...].reshape(cols_in, dt))
     tile[...] = t
@@ -302,8 +294,7 @@
     for k in range(1, n_txt):
         send(row_st.at[txt], (img, p.txt_at(k)), rs_s.at[k - 1], rs_r.at[k - 1])
 
-    for k in range(1, nz):
-        f.line(k)
+    f.line()
     for k in range(1, n_img):
         arrived(col_st.at[p.img_at(n_img - k)], cs_s.at[k - 1], cs_r.at[k - 1])
     for k in range(1, n_txt):
@@ -326,7 +317,6 @@
     tiles[mine, 0:rows_in, :] = both.astype(jnp.bfloat16)
     tiles[mine, rows_in : rows_in + 16, :] = pieces.astype(jnp.bfloat16)
     g.own_z()
-    g.line(0)
 
     def embed(j):
         at = pl.ds(pl.multiple_of(j * cols_in, cols_in), cols_in)
@@ -342,28 +332,23 @@
         e_txt[at, :], i_txt[at, :] = e, inv
         s_txt[at, :] = e.astype(jnp.bfloat16)
 
-    for k in range(nz):
-        f.turn(k)
+    f.turn()
+    g.line()
     f.whole(0)
     for copy in loads[5:]:
         copy.wait()
     embed(txt)
-    for k in range(1, nz):
-        g.line(k)
-    for k in range(nz):
-        f.last(k)
     f.whole(1)
     embed(p.x_txt)
-    for k in range(nz):
-        g.turn(k)
+    f.last()
     f.whole(2)
     embed(p.y_txt)
+    g.turn()
+    g.last()
     f.whole(3)
     embed(p.d_txt)
     outs = [pltpu.make_async_copy(turned, turned_out, load.at[0])]
     outs[0].start()
-    for k in range(nz):
-        g.last(k)
 
     chunks = [slice(c * cols_in, (c + 1) * cols_in) for c in range(n_txt)]
     csm = jnp.full((1, batch), -jnp.inf, jnp.float32)
@@ -403,15 +388,17 @@
         du_img[at, :] = tangent(d_img, e_img[at, :], i_img[at, :]).astype(jnp.bfloat16)
     outs.append(pltpu.make_async_copy(du_img, du_img_out, load.at[1]))
     outs[1].start()
+    parts = jnp.sum(tiles[:, rows_in : rows_in + 16, :].astype(jnp.float32), axis=0)
+    total = total + jnp.sum(terms, axis=1, keepdims=True)
+    total = total + jnp.sum(jnp.sum(parts, axis=0, keepdims=True), axis=1, keepdims=True)
+    loss[...] = total / (2.0 * batch)
+    outs.append(pltpu.make_async_copy(loss, loss_out, load.at[3]))
+    outs[2].start()
     for at in chunks:
         d_txt = dot_tn(g_tile[:, at], s_img[...])
         du_txt[at, :] = tangent(d_txt, e_txt[at, :], i_txt[at, :]).astype(jnp.bfloat16)
     outs.append(pltpu.make_async_copy(du_txt, du_txt_out, load.at[2]))
-    outs[2].start()
-    parts = jnp.sum(tiles[:, rows_in : rows_in + 16, :].astype(jnp.float32), axis=0)
-    total = total + jnp.sum(terms, axis=1, keepdims=True)
-    total = total + jnp.sum(jnp.sum(parts, axis=0, keepdims=True), axis=1, keepdims=True)
-    loss[...] = total / (2.0 * batch)
+    outs[3].start()
     for copy in outs:
         copy.wait()
 
@@ -452,15 +439,15 @@
         pltpu.VMEM((batch, batch), b16),
         dma((7,)),
     ]
-    spread = [(nz - 1,), (nz,), (nz,), (3, nz), (2, nz), (2, nz)]
-    for shape in [(nz - 1,), (nz,), (n_txt - 1,), (n_txt - 1,), (n_img - 1,)] + spread + spread:
+    spread = [(nz - 1,), (4,), (4,)]
+    for shape in [(nz - 1,), (1,), (n_txt - 1,), (n_txt - 1,), (n_img - 1,)] + spread + spread:
         scratch += [dma(shape), dma(shape)]
-    scratch.append(pltpu.VMEM((fi + ft, batch), b16))
+    scratch += [pltpu.VMEM((fi + ft, batch), b16), pltpu.VMEM((1, 1), f32)]
     return pl.pallas_call(
         functools.partial(exchange_kernel, n_img, n_txt),
         out_shape=[jax.ShapeDtypeStruct(*s) for s in outs],
         in_specs=[hbm] * 6,
-        out_specs=[vmem] + [hbm] * 3,
+        out_specs=[hbm] * 4,
         scratch_shapes=scratch,
         compiler_params=pltpu.CompilerParams(
             collective_id=0, has_side_effects=True, vmem_limit_bytes=FUSED_VMEM_BYTES
@@ -480,8 +467,8 @@
     ]
     for copy in loads:
         copy.start()
-    loss[...] = loss_in[...]
-    stores = []
+    stores = [pltpu.make_async_copy(loss_in, loss, store.at[0])]
+    stores[0].start()
 
     def block(lo, at, du, held, out):
         rows = min(step, held.shape[0] - at)
@@ -519,14 +506,14 @@
             jax.ShapeDtypeStruct((fi, ds), f32),
             jax.ShapeDtypeStruct((ft, ds), f32),
         ],
-        in_specs=[vmem] + [hbm] * 3,
-        out_specs=[vmem] + [hbm] * 2,
+        in_specs=[hbm] * 4,
+        out_specs=[hbm] * 3,
         scratch_shapes=[pltpu.VMEM(h.shape, h.dtype) for h in held[1:]]
         + [
             pltpu.VMEM((fi, ds), f32),
             pltpu.VMEM((ft, ds), f32),
             pltpu.SemaphoreType.DMA((4,)),
-            pltpu.SemaphoreType.DMA((pl.cdiv(fi, LANES * 2) + pl.cdiv(ft, LANES * 2),)),
+            pltpu.SemaphoreType.DMA((1 + pl.cdiv(fi, LANES * 2) + pl.cdiv(ft, LANES * 2),)),
         ],
         compiler_params=pltpu.CompilerParams(vmem_limit_bytes=FUSED_VMEM_BYTES),
         name="weight_grads",

time: 35.2 us -> 34.1 us (0.969)
  Pallas kernels: 34.4 us -> 33.3 us
    pallas_call x1, Pallas kernels: 30 us -> 29.4 us  [exchange(): pl.pallas_call(functools.partial(exchange_kernel, n_img, n_txt), out_shap...]
    pallas_call x1, Pallas kernels: 4.45 us -> 3.95 us  [whole_batch(): pl.pallas_call(grads_kernel, out_shape=[jax.ShapeDtypeStruct((1, 1), f32)...]
where the time goes in v5:
time: 34.1 us; the launch traced here: 34 us
  Pallas kernels  33.3 us (98%)
  between operations  0.64 us (2%)
    pallas_call x1, Pallas kernels, exchange(): pl.pallas_call(functools.partial(exchange_kernel, n_img, n_txt), out_shap...  29.4 us
    pallas_call x1, Pallas kernels, whole_batch(): pl.pallas_call(grads_kernel, out_shape=[jax.ShapeDtypeStruct((1, 1), f32)...  3.95 us

profile of v5, /device:TPU:0, one launch (start us, length us, event | category | flops | bytes accessed | tf_op | source)
XLA Modules:
  0.0 34.0 jit_solution(13094848476209961299)
XLA Ops:
  0.6 29.4 %exchange_and_embed.1 = (f32[1,1]{1,0:T(1,128)}, bf16[1280,512]{1,0:T(8,128)(2,1)}, bf16[512,512]{1,0:T(8,128)(2,1)}, bf16[512,512]{1,0:T(8,128)(2,1)}) custom-call(bf16[16,768]{1,0:T(8,128)(2,1)} %image.1, bf16[16,512]{1,0:T(8,128)(2,1)} %text.1, bf16[16,1024]{1,0:T(8,128)(2,1)} %t_img.1, bf16[16,1024]{1,0:T(8,128)(2,1)} %t_txt.1, bf16[768,512]{1,0:T(8,128)(2,1)} %p_img.1, ...), custom_call_target="tpu_custom_call" | custom-call | tf_op jit(solution)/shard_map/exchange_and_embed/pallas_call | solution.py:446
  30.0 3.9 %weight_grads.1 = (f32[1,1]{1,0:T(1,128)}, f32[768,512]{1,0:T(8,128)}, f32[512,512]{1,0:T(8,128)}) custom-call(f32[1,1]{1,0:T(1,128)} %get-tuple-element.10.loss_in, bf16[1280,512]{1,0:T(8,128)(2,1)} %get-tuple-element.11.turned_in, bf16[512,512]{1,0:T(8,128)(2,1)} %get-tuple-element.12.du_img_in, bf16[512,512]{1,0:T(8,128)(2,1)} %get-tuple-element.13.du_txt_in), custom_call_target="tpu_custom_call" | custom-call | tf_op jit(solution)/shard_map/weight_grads/pallas_call | solution.py:502

commit v6 on v5

--- a/solution.py
+++ b/solution.py
@@ -104,7 +104,7 @@
     return lax.dot_general(a, b, (((0,), (0,)), ((), ())), preferred_element_type=jnp.float32)
 
 
-class Spread:
+class LineSpread:
     def __init__(self, place, buf, halves, sems, log, straight=False):
         self.place, self.buf, self.halves, self.log, self.straight = place, buf, halves, log, straight
         self.sz, self.rz, self.sl, self.rl, self.sc, self.rc = sems
@@ -168,6 +168,82 @@
         self.arrived(at, None, self.sc.at[which], self.rc.at[which])
 
 
+class BlockSpread:
+    def __init__(self, place, buf, halves, sems, log, straight=False):
+        self.place, self.buf, self.halves, self.log, self.straight = place, buf, halves, log, straight
+        self.sz, self.rz, self.sx, self.rx, self.sy, self.ry, self.sc, self.rc, self.sd, self.rd, self.se, self.re = sems
+
+    def ref(self, at, part):
+        if part is None:
+            return self.buf.at[at]
+        lo, hi = self.halves[part]
+        return self.buf.at[at, lo:hi]
+
+    def copy(self, at, part, peer, ssem, rsem):
+        ref = self.ref(at, part)
+        return pltpu.make_async_remote_copy(
+            src_ref=ref, dst_ref=ref, send_sem=ssem, recv_sem=rsem, device_id=peer, device_id_type=MESH
+        )
+
+    def send(self, *args):
+        copy = self.copy(*args)
+        copy.start()
+        self.log.append(copy)
+
+    def arrived(self, at, part, ssem, rsem):
+        self.copy(at, part, self.place.partner, ssem, rsem).wait_recv()
+
+    def own_z(self):
+        p = self.place
+        for k in range(1, p.nz):
+            self.send(p.slot(p.img, p.txt), None, p.z_peer(k), self.sz.at[k - 1], self.rz.at[k - 1])
+
+    def line(self, k):
+        p = self.place
+        at = p.slot(p.source(k), p.txt)
+        if k > 0:
+            self.arrived(at, None, self.sz.at[k - 1], self.rz.at[k - 1])
+        self.send(at, None, (p.img, p.x_txt), self.sx.at[k], self.rx.at[k])
+        self.send(at, None, (p.img, p.y_txt), self.sy.at[k], self.ry.at[k])
+        if self.straight:
+            self.send(at, None, (p.img, p.d_txt), self.sd.at[0, k], self.rd.at[0, k])
+        self.send(at, None, p.partner, self.sc.at[0, k], self.rc.at[0, k])
+
+    def turn(self, k):
+        p = self.place
+        at = p.slot(p.source(k), p.x_txt)
+        self.arrived(at, None, self.sx.at[k], self.rx.at[k])
+        if not self.straight:
+            self.send(at, 0, (p.img, p.y_txt), self.sd.at[0, k], self.rd.at[0, k])
+        self.send(at, None, p.partner, self.sc.at[1, k], self.rc.at[1, k])
+        at = p.slot(p.source(k), p.y_txt)
+        self.arrived(at, None, self.sy.at[k], self.ry.at[k])
+        if not self.straight:
+            self.send(at, 1, (p.img, p.x_txt), self.sd.at[1, k], self.rd.at[1, k])
+        self.send(at, None, p.partner, self.sc.at[2, k], self.rc.at[2, k])
+
+    def last(self, k):
+        p = self.place
+        at = p.slot(p.source(k), p.d_txt)
+        for i, part in self.parts():
+            self.arrived(at, part, self.sd.at[i, k], self.rd.at[i, k])
+            self.send(at, part, p.partner, self.se.at[i, k], self.re.at[i, k])
+
+    def parts(self):
+        return ((0, None),) if self.straight else ((0, 0), (1, 1))
+
+    def whole(self, which):
+        p = self.place
+        for k in range(p.nz):
+            source = p.other_source(k)
+            if which < 3:
+                at = p.slot(source, (p.txt, p.x_txt, p.y_txt)[which])
+                self.arrived(at, None, self.sc.at[which, k], self.rc.at[which, k])
+            else:
+                for i, part in self.parts():
+                    self.arrived(p.slot(source, p.d_txt), part, self.se.at[i, k], self.re.at[i, k])
+
+
 class Place:
     def __init__(self, n_img, n_txt):
         self.n_img, self.n_txt, self.nz = n_img, n_txt, n_img // 2
@@ -206,10 +282,10 @@
 def exchange_kernel(n_img, n_txt, image, text, t_img, t_txt, p_img, p_txt, *refs):
     loss_out, turned_out, du_img_out, du_txt_out = refs[:4]
     feats, tiles, e_img, e_txt, i_img, i_txt, s_img, s_txt, sl, ps, du_img, du_txt = refs[4:16]
-    turned, loss = refs[48:50]
+    turned, loss = refs[54:56]
     raw, q_img, q_txt, tile, row_st, col_st, w_img, w_txt, g_tile, load = refs[16:26]
     tz_s, tz_r, tc_s, tc_r, ti_s, ti_r, rs_s, rs_r, cs_s, cs_r = refs[26:36]
-    f_sems, p_sems = refs[36:42], refs[42:48]
+    f_sems, p_sems = refs[36:48], refs[48:54]
     p = Place(n_img, n_txt)
     nz, img, txt = p.nz, p.img, p.txt
     rows, fi = image.shape
@@ -257,18 +333,20 @@
     def arrived(ref, ssem, rsem):
         copy_of(ref, p.partner, ssem, rsem).wait_recv()
 
-    f = Spread(p, feats, ((0, 1), (1, 2)), f_sems, log)
+    f = BlockSpread(p, feats, ((0, 1), (1, 2)), f_sems, log)
     rows_in, cols_in = rows * n_txt, rows * n_img
-    g = Spread(p, tiles, ((0, rows_in // 2), (rows_in // 2, rows_in + 16)), p_sems, log, straight=True)
+    g = LineSpread(p, tiles, ((0, rows_in // 2), (rows_in // 2, rows_in + 16)), p_sems, log, straight=True)
 
     for k in range(1, nz):
         send(q_txt.at[mine_q], p.z_peer(k), tz_s.at[k - 1], tz_r.at[k - 1])
     for k in range(1, n_txt):
         send(q_img.at[txt], (img, p.txt_at(k)), ti_s.at[k - 1], ti_r.at[k - 1])
+    f.line(0)
     for copy in log[: nz - 1]:
         copy.wait_send()
     del log[: nz - 1]
     f.own_z()
+    f.turn(0)
     for k in range(1, nz):
         arrived(q_txt.at[p.order(p.source(k))], tz_s.at[k - 1], tz_r.at[k - 1])
     send(q_txt.at[p.line(img, 0)], p.partner, tc_s.at[0], tc_r.at[0])
@@ -294,7 +372,8 @@
     for k in range(1, n_txt):
         send(row_st.at[txt], (img, p.txt_at(k)), rs_s.at[k - 1], rs_r.at[k - 1])
 
-    f.line()
+    for k in range(1, nz):
+        f.line(k)
     for k in range(1, n_img):
         arrived(col_st.at[p.img_at(n_img - k)], cs_s.at[k - 1], cs_r.at[k - 1])
     for k in range(1, n_txt):
@@ -332,15 +411,17 @@
         e_txt[at, :], i_txt[at, :] = e, inv
         s_txt[at, :] = e.astype(jnp.bfloat16)
 
-    f.turn()
+    for k in range(1, nz):
+        f.turn(k)
     g.line()
     f.whole(0)
     for copy in loads[5:]:
         copy.wait()
     embed(txt)
+    for k in range(nz):
+        f.last(k)
     f.whole(1)
     embed(p.x_txt)
-    f.last()
     f.whole(2)
     embed(p.y_txt)
     g.turn()
@@ -439,8 +520,9 @@
         pltpu.VMEM((batch, batch), b16),
         dma((7,)),
     ]
-    spread = [(nz - 1,), (4,), (4,)]
-    for shape in [(nz - 1,), (1,), (n_txt - 1,), (n_txt - 1,), (n_img - 1,)] + spread + spread:
+    lines = [(nz - 1,), (4,), (4,)]
+    blocks = [(nz - 1,), (nz,), (nz,), (3, nz), (2, nz), (2, nz)]
+    for shape in [(nz - 1,), (1,), (n_txt - 1,), (n_txt - 1,), (n_img - 1,)] + blocks + lines:
         scratch += [dma(shape), dma(shape)]
     scratch += [pltpu.VMEM((fi + ft, batch), b16), pltpu.VMEM((1, 1), f32)]
     return pl.pallas_call(

time: 34.1 us -> 33.9 us (level)
  no operation moved by 1% of the time
where the time goes in v6:
time: 33.9 us; the launch traced here: 33.7 us
  Pallas kernels  33.1 us (98%)
  between operations  0.64 us (2%)
    pallas_call x1, Pallas kernels, exchange(): pl.pallas_call(functools.partial(exchange_kernel, n_img, n_txt), out_shap...  29.2 us
    pallas_call x1, Pallas kernels, whole_batch(): pl.pallas_call(grads_kernel, out_shape=[jax.ShapeDtypeStruct((1, 1), f32)...  3.95 us

profile of v6, /device:TPU:0, one launch (start us, length us, event | category | flops | bytes accessed | tf_op | source)
XLA Modules:
  0.0 33.7 jit_solution(16016784579115633771)
XLA Ops:
  0.6 29.2 %exchange_and_embed.1 = (f32[1,1]{1,0:T(1,128)}, bf16[1280,512]{1,0:T(8,128)(2,1)}, bf16[512,512]{1,0:T(8,128)(2,1)}, bf16[512,512]{1,0:T(8,128)(2,1)}) custom-call(bf16[16,768]{1,0:T(8,128)(2,1)} %image.1, bf16[16,512]{1,0:T(8,128)(2,1)} %text.1, bf16[16,1024]{1,0:T(8,128)(2,1)} %t_img.1, bf16[16,1024]{1,0:T(8,128)(2,1)} %t_txt.1, bf16[768,512]{1,0:T(8,128)(2,1)} %p_img.1, ...), custom_call_target="tpu_custom_call" | custom-call | tf_op jit(solution)/shard_map/exchange_and_embed/pallas_call | solution.py:528
  29.8 3.9 %weight_grads.1 = (f32[1,1]{1,0:T(1,128)}, f32[768,512]{1,0:T(8,128)}, f32[512,512]{1,0:T(8,128)}) custom-call(f32[1,1]{1,0:T(1,128)} %get-tuple-element.10.loss_in, bf16[1280,512]{1,0:T(8,128)(2,1)} %get-tuple-element.11.turned_in, bf16[512,512]{1,0:T(8,128)(2,1)} %get-tuple-element.12.du_img_in, bf16[512,512]{1,0:T(8,128)(2,1)} %get-tuple-element.13.du_txt_in), custom_call_target="tpu_custom_call" | custom-call | tf_op jit(solution)/shard_map/weight_grads/pallas_call | solution.py:584
